TPU v7x, 128 devices: a whole 4x4x4 slice. The times are simulated.
128 devices in a mesh: grp: 16 (over y, x_hi, core), shard: 8 (over z, x_lo).
Axes of the slice: x: 4 (x_hi: 2, x_lo: 2; x = x_hi * 2 + x_lo), y: 4, z: 4, core: 2. Of those that a mesh axis runs over, the one named last changes fastest.
Arguments:
- left_table: float32 [524288, 400], P(('grp', 'shard')), may hold values from -2.4 to 2.4
- right_table: float32 [524288, 400], P(('grp', 'shard')), may hold values from -2.4 to 2.4
- left_state: float32 [524288], P(('grp', 'shard')), may hold values from 0.1 to 4
- right_state: float32 [524288], P(('grp', 'shard')), may hold values from 0.1 to 4
- relations: float32 [1345, 400], replicated, may hold values from -4.2 to 4.2
- relation_state: float32 [1345], replicated, may hold values from 0.1 to 100000
- source_rows: int32 [1152, 1000], P(('grp', 'shard')), may hold values from 0 to 4095
- relation_ids: int32 [1152, 1000], P(('grp', 'shard')), may hold values from 0 to 1344
- target_rows: int32 [1152, 1000], P(('grp', 'shard')), may hold values from 0 to 4095
- negative_rows: int32 [1152, 1000], P(('grp', 'shard')), may hold values from 0 to 4095
- span_sizes: int32 [128, 9], P(('grp', 'shard')), may hold values from 1 to 1000, 6750 in all within a row
Outputs:
- new_left: float32 [524288, 400], P(('grp', 'shard'))
- new_left_state: float32 [524288], P(('grp', 'shard'))
- new_right: float32 [524288, 400], P(('grp', 'shard'))
- new_right_state: float32 [524288], P(('grp', 'shard'))
- new_relations: float32 [1345, 400], replicated
- new_relation_state: float32 [1345], replicated
Inputs may be any that keep to these rules, and one draw needn't show every extreme that they name: `source_rows`: local row ids of the device's own source-side rows. `target_rows`: local row ids of the device's own target-side rows. `negative_rows`: negative j of a span names a local row of device j // 125 of the same group; rows may repeat. The first span_sizes edges of a span are live.
All inputs are finite; a program needn't handle non-finite values.
Results may differ from a plain program's by a relative error of at most 0.0017.
Values may be sent and summed in bfloat16 or wider, within the bound.
A program may use at most 256 MiB of HBM per device.

v0:
```python
import jax
import jax.numpy as jnp
from jax import lax
from jax.sharding import PartitionSpec as P

ROUND = 5


LEARN_RATE = 0.1
EPSILON = 1e-08


def passed_along(block, axis, distance):
    devices = range(lax.axis_size(axis))
    route = [((i - distance) % len(devices), i) for i in devices]
    return lax.ppermute(block, axis, route)


def complex_mul(left, right):
    middle = left.shape[-1] // 2
    left_real, left_imag = (left[..., :middle], left[..., middle:])
    right_real, right_imag = (right[..., :middle], right[..., middle:])
    return jnp.concatenate(
        [
            left_real * right_real - left_imag * right_imag,
            left_real * right_imag + left_imag * right_real,
        ],
        -1,
    )


def conj_mul(grad, other):
    middle = grad.shape[-1] // 2
    grad_real, grad_imag = (grad[..., :middle], grad[..., middle:])
    other_real, other_imag = (other[..., :middle], other[..., middle:])
    return jnp.concatenate(
        [
            grad_real * other_real + grad_imag * other_imag,
            grad_imag * other_real - grad_real * other_imag,
        ],
        -1,
    )


def span_terms(source, relation, target, negatives, weights):
    product = complex_mul(source, relation)
    product_b = product.astype(jnp.bfloat16)
    positive = jnp.sum(product * target, -1)
    scores = lax.dot_general(
        product_b, negatives, (((1,), (1,)), ((), ())), preferred_element_type=jnp.float32
    )
    pos_grad = -jax.nn.sigmoid(-positive) * weights
    neg_grad = (jax.nn.sigmoid(scores) * weights[:, None]).astype(jnp.bfloat16)
    grad_product = pos_grad[:, None] * target + jnp.dot(
        neg_grad, negatives, preferred_element_type=jnp.float32
    )
    grad_target = pos_grad[:, None] * product
    grad_negatives = lax.dot_general(
        neg_grad, product_b, (((0,), (0,)), ((), ())), preferred_element_type=jnp.float32
    ).astype(jnp.bfloat16)
    grad_source = conj_mul(grad_product, relation)
    grad_relation = conj_mul(grad_product, source)
    return (grad_source, grad_relation, grad_target, grad_negatives)


def row_adagrad(table, state, grad):
    new_state = state + jnp.mean(grad * grad, -1)
    return (table - LEARN_RATE * grad / (jnp.sqrt(new_state)[:, None] + EPSILON), new_state)


def local(
    left_table,
    right_table,
    left_state,
    right_state,
    relations,
    relation_state,
    source_rows,
    relation_ids,
    target_rows,
    negative_rows,
    span_sizes,
):
    shards = lax.axis_size("shard")
    spans, span_len = source_rows.shape
    neg_count = negative_rows.shape[1]
    neg_per = neg_count // shards
    width = left_table.shape[1]
    asked = lax.all_to_all(
        negative_rows.reshape(spans, shards, neg_per),
        "shard",
        split_axis=1,
        concat_axis=1,
        tiled=True,
    )
    served = right_table[asked].astype(jnp.bfloat16)
    fetched = lax.all_to_all(served, "shard", split_axis=1, concat_axis=1, tiled=True).reshape(
        spans, neg_count, width
    )
    positions = jnp.arange(span_len, dtype=jnp.int32)

    def step(carry, inputs):
        grad_left, grad_right, grad_rel = carry
        sources, kinds, targets, negatives, live = inputs
        weights = (positions < live).astype(jnp.float32)
        source = left_table[sources]
        relation = relations[kinds]
        target = right_table[targets]
        grad_source, grad_relation, grad_target, grad_negatives = span_terms(
            source, relation, target, negatives, weights
        )
        grad_left = grad_left.at[sources].add(grad_source)
        grad_right = grad_right.at[targets].add(grad_target)
        grad_rel = grad_rel.at[kinds].add(grad_relation)
        return ((grad_left, grad_right, grad_rel), grad_negatives)

    start = (
        jnp.zeros(left_table.shape, jnp.float32),
        jnp.zeros(right_table.shape, jnp.float32),
        jnp.zeros(relations.shape, jnp.float32),
    )
    totals, neg_grads = lax.scan(
        step, start, (source_rows, relation_ids, target_rows, fetched, span_sizes[0])
    )
    grad_left, grad_right, grad_rel = totals
    new_left, new_left_state = row_adagrad(left_table, left_state, grad_left)
    returned = lax.all_to_all(
        neg_grads.reshape(spans, shards, neg_per, width),
        "shard",
        split_axis=1,
        concat_axis=1,
        tiled=True,
    )
    grad_right = grad_right.at[asked.reshape(-1)].add(
        returned.reshape(-1, width).astype(jnp.float32)
    )
    rel_total = lax.psum(grad_rel, ("grp", "shard"))
    new_right, new_right_state = row_adagrad(right_table, right_state, grad_right)
    new_relations, new_relation_state = row_adagrad(relations, relation_state, rel_total)
    moved = passed_along((new_left, new_left_state, new_right, new_right_state), "grp", ROUND)
    return (moved[0], moved[1], moved[2], moved[3], new_relations, new_relation_state)


def solution(mesh):
    placed = (
        P(("grp", "shard"), None),
        P(("grp", "shard"), None),
        P(("grp", "shard")),
        P(("grp", "shard")),
        P(),
        P(),
        P(("grp", "shard"), None),
        P(("grp", "shard"), None),
        P(("grp", "shard"), None),
        P(("grp", "shard"), None),
        P(("grp", "shard"), None),
    )
    return jax.shard_map(
        local,
        mesh=mesh,
        in_specs=placed,
        out_specs=(
            P(("grp", "shard"), None),
            P(("grp", "shard")),
            P(("grp", "shard"), None),
            P(("grp", "shard")),
            P(),
            P(),
        ),
        check_vma=False,
    )
```

profile of v0, /device:TPU:1, one launch (start us, length us, event | category | flops | bytes accessed | tf_op | source)
XLA Modules:
  0.0 1698.9 jit_solution(17855991335586274182)
XLA Ops:
  15.5 8.5 copy.173
  24.3 30.1 %gather_fusion.3 = bf16[9000,400]{1,0:T(8,128)(2,1)} fusion(f32[4096,400]{1,0:T(8,128)} %copy.173, s32[9216]{0:T(1024)S(1)} %pad_clamp_fusion.3), kind=kCustom, calls=%fused_computation.3 | custom fusion | bytes 14436000 | tf_op jit(solution)/shard_map/gather | solution.py:96
  54.4 11.3 copy.168
  65.6 14.9 reshape.229
  95.0 8.5 copy.175
  103.5 71.4 %all-to-all-done.1 = bf16[9,8,125,400]{2,3,0,1:T(8,128)(2,1)} async-done(((bf16[9,8,125,400]{2,3,0,1:T(8,128)(2,1)}), bf16[9,8,125,400]{2,3,0,1:T(8,128)(2,1)}, u32[]{:S(2)}, u32[]{:S(2)}) %all-to-all-start.1) | async-done | bytes 7200032 | tf_op jit(solution)/shard_map/all_to_all | solution.py:97
  174.9 11.7 copy.184
  186.6 12.5 reshape.245
  208.1 1021.6 %while.17 = (s32[]{:T(128)}, f32[4096,400]{1,0:T(8,128)}, f32[4096,400]{1,0:T(8,128)}, f32[1345,400]{1,0:T(8,128)S(1)}, bf16[9,1000,400]{1,2,0:T(8,128)(2,1)}, /...) while((s32[]{:T(128)}, f32[4096,400]{1,0:T(8,128)}, ...), condition=%wide.region_5.6_spmd.clone, body=%wide.region_0.5_spmd.clone.sunk | while | flops 2417018112 | bytes 130692728 | solution.py:122
  211.2 8.6 gather_fusion.1
  237.9 8.6 gather_fusion
  281.0 8.2 scatter_fusion.2
  293.3 13.8 scatter_fusion
  307.1 13.8 scatter_fusion.1
  323.8 8.6 gather_fusion.1
  350.5 8.6 gather_fusion
  393.6 8.2 scatter_fusion.2
  405.7 13.8 scatter_fusion
  419.5 13.8 scatter_fusion.1
  436.2 8.6 gather_fusion.1
  462.9 8.6 gather_fusion
  506.0 8.2 scatter_fusion.2
  518.2 13.8 scatter_fusion
  532.0 13.8 scatter_fusion.1
  548.7 8.6 gather_fusion.1
  575.4 8.6 gather_fusion
  618.5 8.2 scatter_fusion.2
  630.7 13.8 scatter_fusion
  644.5 13.8 scatter_fusion.1
  661.1 8.6 gather_fusion.1
  687.8 8.6 gather_fusion
  730.9 8.2 scatter_fusion.2
  743.1 13.8 scatter_fusion
  756.9 13.8 scatter_fusion.1
  773.6 8.6 gather_fusion.1
  800.3 8.6 gather_fusion
  843.4 8.2 scatter_fusion.2
  855.6 13.8 scatter_fusion
  869.5 13.8 scatter_fusion.1
  886.1 8.6 gather_fusion.1
  912.8 8.6 gather_fusion
  968.1 13.8 scatter_fusion
  981.9 13.8 scatter_fusion.1
  998.6 8.6 gather_fusion.1
  1025.3 8.6 gather_fusion
  1068.4 8.2 scatter_fusion.2
  1080.6 13.8 scatter_fusion
  1094.4 13.8 scatter_fusion.1
  1111.0 8.6 gather_fusion.1
  1137.8 8.6 gather_fusion
  1180.9 8.2 scatter_fusion.2
  1193.0 13.8 scatter_fusion
  1206.8 13.8 scatter_fusion.1
  1229.7 15.2 reshape.161
  1261.6 10.0 divide_subtract_fusion.1
  1271.6 8.5 copy.176
  1285.9 52.3 %all-to-all-done.2 = bf16[9,8,125,400]{2,3,0,1:T(8,128)(2,1)} async-done(((bf16[9,8,125,400]{2,3,0,1:T(8,128)(2,1)}), bf16[9,8,125,400]{2,3,0,1:T(8,128)(2,1)}, u32[]{:S(2)}, u32[]{:S(2)}) %all-to-all-start.2) | async-done | bytes 7200032 | tf_op jit(solution)/shard_map/all_to_all | solution.py:127
  1338.2 13.2 copy.185
  1351.5 16.8 reshape.246
  1368.2 61.8 %scatter_fusion.3 = f32[4096,400]{1,0:T(8,128)} fusion(f32[4096,400]{1,0:T(8,128)} %get-tuple-element.82, s32[9000]{0:T(1024)S(1)} %fusion.18, f32[9000,400]{1,0:T(8,128)} %reshape.246), kind=kCustom, calls=%fused_computation.7 | custom fusion | flops 3600000 | bytes 43236000 | tf_op jit(solution)/shard_map/scatter-add | solution.py:134
  1441.9 8.5 copy.182
  1450.5 9.7 collective-permute-start.2
  1462.3 144.1 %collective-permute-done.1 = f32[4096]{0:T(1024)S(1)} collective-permute-done((f32[4096]{0:T(1024)S(1)}, f32[4096]{0:T(1024)S(1)}, u32[]{:S(2)}, u32[]{:S(2)}) %collective-permute-start.1) | collective-permute-done | bytes 16416 | tf_op jit(solution)/shard_map/ppermute | solution.py:16
  1606.4 64.5 %all-reduce.2.cloned.1.call-done = f32[1345,400]{0,1:T(8,128)} async-done(((f32[1345,400]{0,1:T(8,128)}), f32[1345,400]{0,1:T(8,128)}) %all-reduce.2.cloned.1.call-update) | async-done | bytes 2152016 | tf_op jit(solution)/shard_map/psum | solution.py:137
  (476 shorter events, 630.0 us)
Async XLA Ops:
  8.7 15.3 all-to-all-start
  24.1 30.3 %copy-start.12 = (s32[9,8,125]{2,0,1:T(8,128)}, s32[9,8,125]{2,0,1:T(8,128)S(1)}, u32[]{:S(2)}) copy-start(s32[9,8,125]{2,0,1:T(8,128)S(1)} %all-to-all-done) | copy-start | bytes 108004
  87.5 5.3 copy-start.9
  87.5 87.4 %all-to-all-start.1 = ((bf16[9,8,125,400]{2,3,0,1:T(8,128)(2,1)}), bf16[9,8,125,400]{2,3,0,1:T(8,128)(2,1)}, u32[]{:S(2)}, u32[]{:S(2)}) async-start(bf16[9,8,125,400]{2,3,0,1:T(8,128)(2,1)} %copy.169), calls=%async_computation.1 | async-start | bytes 14745600 | tf_op jit(solution)/shard_map/all_to_all | solution.py:97
  203.8 4.3 copy-start.17
  262.5 3.8 copy-start.8
  266.3 3.1 copy-start.18
  266.3 3.1 copy-start.3
  266.3 3.1 copy-start.4
  266.3 3.1 copy-start.5
  266.3 3.1 copy-start.6
  375.0 3.8 copy-start.8
  378.8 3.1 copy-start.18
  378.8 3.1 copy-start.3
  378.8 3.1 copy-start.4
  378.8 3.1 copy-start.5
  378.8 3.1 copy-start.6
  487.4 3.8 copy-start.8
  491.2 3.1 copy-start.18
  491.3 3.1 copy-start.3
  491.3 3.1 copy-start.4
  491.3 3.1 copy-start.5
  491.3 3.1 copy-start.6
  599.9 3.8 copy-start.8
  603.7 3.1 copy-start.18
  603.7 3.1 copy-start.3
  712.4 3.8 copy-start.8
  716.2 3.1 copy-start.18
  716.2 3.1 copy-start.3
  716.2 3.1 copy-start.4
  716.2 3.1 copy-start.5
  716.2 3.1 copy-start.6
  824.8 3.8 copy-start.8
  828.6 3.1 copy-start.18
  828.7 3.1 copy-start.3
  828.7 3.1 copy-start.4
  828.7 3.1 copy-start.5
  828.7 3.1 copy-start.6
  937.3 3.8 copy-start.8
  1049.8 3.8 copy-start.8
  1053.6 3.1 copy-start.18
  1053.6 3.1 copy-start.3
  1053.6 3.1 copy-start.4
  1053.6 3.1 copy-start.5
  1053.7 3.1 copy-start.6
  1162.3 3.8 copy-start.8
  1166.1 3.1 copy-start.18
  1166.1 3.1 copy-start.3
  1166.1 3.1 copy-start.4
  1166.1 3.1 copy-start.5
  1166.1 3.1 copy-start.6
  1252.1 5.1 copy-start.13
  1252.1 86.2 %all-to-all-start.2 = ((bf16[9,8,125,400]{2,3,0,1:T(8,128)(2,1)}), bf16[9,8,125,400]{2,3,0,1:T(8,128)(2,1)}, u32[]{:S(2)}, u32[]{:S(2)}) async-start(bf16[9,8,125,400]{2,3,0,1:T(8,128)(2,1)} %copy.178), calls=%async_computation.2 | async-start | bytes 14745600 | tf_op jit(solution)/shard_map/all_to_all | solution.py:127
  1257.1 413.8 %all-reduce.2.cloned.1.call-start = ((), (), s32[]{:S(2)}) async-start(), calls=%async_computation.3 | async-start | bytes 4505600 | tf_op jit(solution)/shard_map/psum | solution.py:137
  1257.5 4.1 copy-start.14
  1280.2 397.7 %collective-permute-start = (f32[4096,400]{0,1:T(8,128)}, f32[4096,400]{0,1:T(8,128)}, u32[]{:S(2)}, u32[]{:S(2)}) collective-permute-start(f32[4096,400]{0,1:T(8,128)} %copy.176), channel_id=1, source_target_pairs={{88,0},{96,8},{104,16},{112,24},{120,32},{0,40},{8,48},{16,56},{24... | collective-permute-start | bytes 19660808 | tf_op jit(solution)/shard_map/ppermute | solution.py:16
  1430.0 4.2 copy-start.15
  1430.0 5.8 copy-start
  1450.5 227.4 %collective-permute-start.2 = (f32[4096,400]{0,1:T(8,128)}, f32[4096,400]{0,1:T(8,128)}, u32[]{:S(2)}, u32[]{:S(2)}) collective-permute-start(f32[4096,400]{0,1:T(8,128)} %copy.182), channel_id=1, source_target_pairs={{88,0},{96,8},{104,16},{112,24},{120,32},{0,40},{8,48},{16,56},{24... | collective-permute-start | bytes 19660808 | tf_op jit(solution)/shard_map/ppermute | solution.py:16
  1462.2 210.7 %copy-start.16 = (f32[1345]{0:T(1024)S(1)}, f32[1345]{0:T(1024)}, u32[]{:S(2)}) copy-start(f32[1345]{0:T(1024)} %param.18) | copy-start | bytes 16144
  1462.2 213.1 %copy-start.10 = (f32[1345,400]{0,1:T(8,128)S(1)}, f32[1345,400]{0,1:T(8,128)}, u32[]{:S(2)}) copy-start(f32[1345,400]{0,1:T(8,128)} %param.17) | copy-start | bytes 6456004
  1462.3 144.2 %collective-permute-start.1 = (f32[4096]{0:T(1024)S(1)}, f32[4096]{0:T(1024)S(1)}, u32[]{:S(2)}, u32[]{:S(2)}) collective-permute-start(f32[4096]{0:T(1024)S(1)} %get-tuple-element.247), channel_id=1, source_target_pairs={{88,0},{96,8},{104,16},{112,24},{120,32},{0,40},{8,48},{16,56},{24... | collective-permute-start | bytes 49160 | tf_op jit(solution)/shard_map/ppermute | solution.py:16
  1670.9 4.4 copy-start.11
  1673.5 4.4 collective-permute-start.3
  (35 other events, 67.3 us)
Sparse Core Ops, SparseCore 0:
  1462.4 208.4 all-reduce.1
where the time goes:
time: 1720 us; the launch traced here: 1700 us
  local copies, waits for them, and re-layouts  679 us (39%)
  other arithmetic  530 us (31%)
  waiting for transfers between devices  333 us (19%)
  matrix products  97.1 us (6%)
  starting transfers between devices  34.5 us (2%)
    ppermute x4, waiting for transfers between devices, passed_along(): return lax.ppermute(block, axis, route)  145 us
    scatter-add x9, other arithmetic, step(): grad_right = grad_right.at[targets].add(grad_target)  124 us
    scatter-add x9, other arithmetic, step(): grad_left = grad_left.at[sources].add(grad_source)  124 us
    gather x18, local copies, waits for them, and re-layouts, step(): target = right_table[targets]  103 us
    while x198, local copies, waits for them, and re-layouts  89.4 us
    gather x9, local copies, waits for them, and re-layouts, step(): source = left_table[sources]  77.7 us
    scatter-add x9, other arithmetic, step(): grad_rel = grad_rel.at[kinds].add(grad_relation)  74.1 us
    all_to_all x1, waiting for transfers between devices, local(): lax.all_to_all(served, 'shard', split_axis=1, concat_axis=1, tiled=True)  71.4 us
  transfers between devices with their start and end apart: 8, of which 5 were waited for; matrix products, arithmetic and copies ran while one was open for 9% of the time, Pallas kernels for 0%

commit v1 on v0

v1 whole, which is shorter than its diff:
```python
import functools

import jax
import jax.numpy as jnp
from jax import lax
from jax.experimental import pallas as pl
from jax.experimental.pallas import tpu as pltpu
from jax.sharding import PartitionSpec as P

ROUND = 5
LEARN_RATE = 0.1
EPSILON = 1e-08

WIDTH = 400
HALF = 200
REST = HALF - 128
SPANS = 9
PEERS = 8
NEG_PER = 125
SLOT = 128
SPAN_PAD = 1024
ROWS = 4096
DUMP = ROWS
TALL = 4 * (ROWS + 8)
RELS = 1345
RELS_PAD = 1408
CORES = 2
CHIPS = 8
REL_SHARE = 48
REL_TALL = CORES * PEERS * CHIPS * REL_SHARE
PARTS = 1
PART = SPANS // PARTS
TILE = 256
SUB = 32
UNROLL = 16
CHUNKS = ((0, 128), (128, 200), (200, 328), (328, 400))
WIRE = 400

F32 = jnp.float32
BF16 = jnp.bfloat16
PARAMS = dict(vmem_limit_bytes=58 * 1024 * 1024)


def lane_ids(shape):
    return lax.broadcasted_iota(jnp.int32, shape, len(shape) - 1)


def to_rows(t_ref, out_ref, count):
    def block(i, _):
        at = pl.ds(pl.multiple_of(i * 128, 128), 128)
        for c, (low, high) in enumerate(CHUNKS):
            part = t_ref[low:high, at]
            if high - low < 128:
                part = jnp.concatenate([part, jnp.zeros((128 - (high - low), 128), F32)], 0)
            out_ref[pl.ds(i * 512 + c, 128, stride=4), :] = part.T
        return 0

    lax.fori_loop(0, count // 128, block, 0)


def adagrad_block(g_ref, t, state, i):
    parts = []
    for c, (low, high) in enumerate(CHUNKS):
        part = g_ref[pl.ds(i * 512 + c, 128, stride=4), :].T
        parts.append(part[: high - low])
    grad = jnp.concatenate(parts, 0)
    new_state = state + jnp.sum(grad * grad, 0, keepdims=True) * (1.0 / WIDTH)
    rate = LEARN_RATE / (jnp.sqrt(new_state) + EPSILON)
    return t - grad * rate, new_state


def adagrad_tables(g_ref, t_ref, state_ref, new_ref, new_state_ref):
    def block(i, _):
        at = pl.ds(pl.multiple_of(i * 128, 128), 128)
        new, state = adagrad_block(g_ref, t_ref[:, at], state_ref[:, at], i)
        new_ref[:, at] = new.astype(new_ref.dtype)
        new_state_ref[:, at] = state
        return 0

    lax.fori_loop(0, ROWS // 128, block, 0)


def spot(group, j):
    return pl.ds(group * (4 * UNROLL) + (j // 8) * 32 + (j % 8), 4, stride=8)


def row(index):
    return pl.ds(pl.multiple_of(index * 4, 4), 4)


def serve_kernel(ids, t_ref, out_ref, table, stage):
    peer = pl.program_id(0)

    @pl.when(peer == 0)
    def _():
        to_rows(t_ref, table, ROWS)
        table[4 * ROWS :, :] = jnp.zeros((TALL - 4 * ROWS, 128), F32)

    lanes = lane_ids((SLOT, 128))

    def span(c, _):
        base = peer * (SPANS * SLOT) + c * SLOT

        def group(g, _):
            for j in range(UNROLL):
                stage[spot(g, j), :] = table[row(ids[base + g * UNROLL + j]), :]
            return 0

        lax.fori_loop(0, SLOT // UNROLL, group, 0)
        s = stage[...].reshape(SLOT // 8, 4, 8, 128)
        re0, re1, im0, im1 = (s[:, k].reshape(SLOT, 128) for k in range(4))
        moved = pltpu.roll(im1, REST, 1)
        mixed = jnp.where(lanes < REST, re1, moved)
        tail = jnp.where(lanes < 16, moved, 0.0)
        packed = tail[:16]
        for k in range(1, 8):
            packed = packed + pltpu.roll(tail[16 * k : 16 * k + 16], 16 * k, 1)
        at = pl.multiple_of(c * WIRE, 16)
        out_ref[0, pl.ds(at, 128), :] = re0.astype(BF16)
        out_ref[0, pl.ds(at + 128, 128), :] = im0.astype(BF16)
        out_ref[0, pl.ds(at + 256, 128), :] = mixed.astype(BF16)
        out_ref[0, pl.ds(at + 384, 16), :] = packed.astype(BF16)
        return 0

    lax.fori_loop(0, SPANS, span, 0)


def serve(ids, table_t):
    return pl.pallas_call(
        serve_kernel,
        grid=(PEERS,),
        out_shape=jax.ShapeDtypeStruct((PEERS, SPANS * WIRE, 128), BF16),
        in_specs=[
            pl.BlockSpec(memory_space=pltpu.SMEM),
            pl.BlockSpec(memory_space=pltpu.VMEM),
        ],
        out_specs=pl.BlockSpec((1, SPANS * WIRE, 128), lambda p: (p, 0, 0)),
        scratch_shapes=[
            pltpu.VMEM((TALL, 128), F32),
            pltpu.VMEM((4 * SLOT, 128), F32),
        ],
        compiler_params=pltpu.CompilerParams(**PARAMS),
        cost_estimate=pl.CostEstimate(flops=0, bytes_accessed=80_000_000, transcendentals=0),
        name="serve",
    )(ids, table_t)


def unpack_wire(block):
    lanes = lane_ids((SLOT, 128))
    re0, im0, mixed, packed = block[:128], block[128:256], block[256:384], block[384:400]
    re1 = jnp.where(lanes < REST, mixed, 0.0)
    tail = jnp.concatenate([pltpu.roll(packed, (56 - 16 * k) % 128, 1) for k in range(8)], 0)
    im1 = jnp.where(lanes < 56, pltpu.roll(mixed, 56, 1), jnp.where(lanes < REST, tail, 0.0))
    return re0, re1, im0, im1


def forward_kernel(
    src, rel, tgt, live_ref, left_t, right_t, rel_t,
    s_out, b_out, p_out, pt_out, g_ref,
    left, right, rels, s_st, b_st, t_st, g_st,
):
    c = pl.program_id(0)

    @pl.when(c == 0)
    def _():
        to_rows(left_t, left, ROWS)
        to_rows(right_t, right, ROWS)
        to_rows(rel_t, rels, RELS_PAD)
        g_ref[...] = jnp.zeros_like(g_ref)
        for st in (s_st, b_st, t_st):
            st[...] = jnp.zeros_like(st)

    live = live_ref[c]

    def tile(t, _):
        base = c * SPAN_PAD + t * TILE
        left_over = jnp.minimum(live - t * TILE, TILE)
        groups = (left_over + UNROLL - 1) // UNROLL

        def gather(g, _):
            for j in range(UNROLL):
                e = base + g * UNROLL + j
                s_st[spot(g, j), :] = left[row(src[e]), :]
                b_st[spot(g, j), :] = rels[row(rel[e]), :]
                t_st[spot(g, j), :] = right[row(tgt[e]), :]
            return 0

        lax.fori_loop(0, groups, gather, 0)

        def sub(k, _):
            at = pl.ds(pl.multiple_of(k * (4 * SUB), 4 * SUB), 4 * SUB)
            s, b, q = (st[at, :].reshape(SUB // 8, 4, 8, 128) for st in (s_st, b_st, t_st))
            re = [s[:, i] * b[:, i] - s[:, i + 2] * b[:, i + 2] for i in range(2)]
            im = [s[:, i] * b[:, i + 2] + s[:, i + 2] * b[:, i] for i in range(2)]
            prod = re + im
            positive = jnp.sum(
                prod[0] * q[:, 0] + prod[1] * q[:, 1] + prod[2] * q[:, 2] + prod[3] * q[:, 3],
                -1, keepdims=True,
            )
            shape = (SUB // 8, 8, 1)
            where = (
                k * SUB
                + lax.broadcasted_iota(jnp.int32, shape, 0) * 8
                + lax.broadcasted_iota(jnp.int32, shape, 1)
            )
            pos_grad = jnp.where(where < left_over, -jax.nn.sigmoid(-positive), 0.0)
            g_st[at, :] = jnp.stack([pos_grad * x for x in prod], 1).reshape(4 * SUB, 128)
            rows = pl.ds(pl.multiple_of(t * TILE + k * SUB, SUB), SUB)
            for i in range(4):
                lanes = slice(i * 128, i * 128 + 128)
                s_out[0, rows, lanes] = s[:, i].reshape(SUB, 128).astype(BF16)
                b_out[0, rows, lanes] = b[:, i].reshape(SUB, 128).astype(BF16)
                p_out[0, rows, lanes] = prod[i].reshape(SUB, 128).astype(BF16)
                pt_out[0, rows, lanes] = (pos_grad * q[:, i]).reshape(SUB, 128).astype(BF16)
            return 0

        lax.fori_loop(0, TILE // SUB, sub, 0)

        def scatter(g, _):
            for j in range(UNROLL):
                at = row(tgt[base + g * UNROLL + j])
                g_ref[at, :] = g_ref[at, :] + g_st[spot(g, j), :]
            return 0

        lax.fori_loop(0, groups, scatter, 0)
        return 0

    lax.fori_loop(0, (live + TILE - 1) // TILE, tile, 0)


def forward(src, rel, tgt, live, left_t, right_t, rel_t):
    smem = pl.BlockSpec(memory_space=pltpu.SMEM)
    vmem = pl.BlockSpec(memory_space=pltpu.VMEM)
    per_edge = jax.ShapeDtypeStruct((SPANS, SPAN_PAD, 512), BF16)
    block = pl.BlockSpec((1, SPAN_PAD, 512), lambda c: (c, 0, 0))
    stage = pltpu.VMEM((4 * TILE, 128), F32)
    return pl.pallas_call(
        forward_kernel,
        grid=(SPANS,),
        out_shape=[per_edge] * 4 + [jax.ShapeDtypeStruct((4 * ROWS, 128), F32)],
        in_specs=[smem] * 4 + [vmem] * 3,
        out_specs=[block] * 4 + [vmem],
        scratch_shapes=[
            pltpu.VMEM((4 * ROWS, 128), F32),
            pltpu.VMEM((4 * ROWS, 128), F32),
            pltpu.VMEM((4 * RELS_PAD, 128), F32),
        ]
        + [stage] * 4,
        compiler_params=pltpu.CompilerParams(**PARAMS),
        cost_estimate=pl.CostEstimate(flops=0, bytes_accessed=280_000_000, transcendentals=0),
        name="forward",
    )(src, rel, tgt, live, left_t, right_t, rel_t)


def negatives_kernel(first, live_ref, p_ref, pt_ref, got_ref, *rest):
    gp_ref, back_ref, neg, acc = rest[-4:]
    c = pl.program_id(0)
    live = live_ref[first + c]

    def unpack(p, _):
        block = got_ref[p].astype(F32)
        at = pl.ds(pl.multiple_of(p * SLOT, SLOT), SLOT)
        for k, part in enumerate(unpack_wire(block)):
            neg[at, k * 128 : k * 128 + 128] = part.astype(BF16)
        return 0

    lax.fori_loop(0, PEERS, unpack, 0)
    acc[...] = jnp.zeros_like(acc)

    def tile(t, _):
        rows = pl.ds(pl.multiple_of(t * TILE, TILE), TILE)
        product = p_ref[0, rows, :]
        scores = lax.dot_general(
            product, neg[...], (((1,), (1,)), ((), ())), preferred_element_type=F32
        )
        where = t * TILE + lax.broadcasted_iota(jnp.int32, (TILE, 1), 0)
        weight = (where < live).astype(F32) * 0.5
        grad = (weight * jnp.tanh(scores * 0.5) + weight).astype(BF16)
        gp = jnp.dot(grad, neg[...], preferred_element_type=F32)
        gp_ref[0, rows, :] = (gp + pt_ref[0, rows, :].astype(F32)).astype(BF16)
        acc[...] += lax.dot_general(
            grad, product, (((0,), (0,)), ((), ())), preferred_element_type=F32
        )
        return 0

    lax.fori_loop(0, (live + TILE - 1) // TILE, tile, 0)

    lanes = lane_ids((SLOT, 128))

    def pack(p, _):
        g = acc[pl.ds(pl.multiple_of(p * SLOT, SLOT), SLOT), :]
        re0, re1, im0, im1 = (g[:, k * 128 : k * 128 + 128] for k in range(4))
        moved = pltpu.roll(im1, REST, 1)
        tail = jnp.where(lanes < 16, moved, 0.0)
        packed = tail[:16]
        for k in range(1, 8):
            packed = packed + pltpu.roll(tail[16 * k : 16 * k + 16], 16 * k, 1)
        back_ref[p, 0:128, :] = re0.astype(BF16)
        back_ref[p, 128:256, :] = im0.astype(BF16)
        back_ref[p, 256:384, :] = jnp.where(lanes < REST, re1, moved).astype(BF16)
        back_ref[p, 384:400, :] = packed.astype(BF16)
        return 0

    lax.fori_loop(0, PEERS, pack, 0)


def negatives(live, product, pos_target, got, first, grad_product):
    block = pl.BlockSpec((1, SPAN_PAD, 512), lambda c: (first + c, 0, 0))
    wire = pl.BlockSpec((PEERS, WIRE, 128), lambda c: (0, first + c, 0))
    operands = [live, product, pos_target, got]
    specs = [pl.BlockSpec(memory_space=pltpu.SMEM), block, block, wire]
    aliases = {}
    if grad_product is not None:
        operands.append(grad_product)
        specs.append(pl.BlockSpec(memory_space=pl.ANY))
        aliases = {4: 0}
    return pl.pallas_call(
        functools.partial(negatives_kernel, first),
        grid=(PART,),
        out_shape=[
            jax.ShapeDtypeStruct((SPANS, SPAN_PAD, 512), BF16),
            jax.ShapeDtypeStruct((PEERS, PART * WIRE, 128), BF16),
        ],
        in_specs=specs,
        out_specs=[block, pl.BlockSpec((PEERS, WIRE, 128), lambda c: (0, c, 0))],
        scratch_shapes=[
            pltpu.VMEM((PEERS * SLOT, 512), BF16),
            pltpu.VMEM((PEERS * SLOT, 512), F32),
        ],
        input_output_aliases=aliases,
        compiler_params=pltpu.CompilerParams(**PARAMS),
        cost_estimate=pl.CostEstimate(
            flops=14_000_000_000, bytes_accessed=60_000_000, transcendentals=3_000_000
        ),
        name="negatives",
    )(*operands)


def left_kernel(
    src, rel, live_ref, s_ref, b_ref, gp_ref, left_t, state, new_ref, new_state, rel_out, gleft, grel, a_st, r_st
):
    c = pl.program_id(0)

    @pl.when(c == 0)
    def _():
        gleft[...] = jnp.zeros_like(gleft)
        grel[...] = jnp.zeros_like(grel)

    live = live_ref[c]

    def tile(t, _):
        base = c * SPAN_PAD + t * TILE
        groups = (jnp.minimum(live - t * TILE, TILE) + UNROLL - 1) // UNROLL

        def sub(k, _):
            rows = pl.ds(pl.multiple_of(t * TILE + k * SUB, SUB), SUB)
            s, b, g = (
                [
                    ref[0, rows, i * 128 : i * 128 + 128].astype(F32).reshape(SUB // 8, 8, 128)
                    for i in range(4)
                ]
                for ref in (s_ref, b_ref, gp_ref)
            )
            at = pl.ds(pl.multiple_of(k * (4 * SUB), 4 * SUB), 4 * SUB)
            for st, o in ((a_st, b), (r_st, s)):
                re = [g[i] * o[i] + g[i + 2] * o[i + 2] for i in range(2)]
                im = [g[i + 2] * o[i] - g[i] * o[i + 2] for i in range(2)]
                st[at, :] = jnp.stack(re + im, 1).reshape(4 * SUB, 128)
            return 0

        lax.fori_loop(0, TILE // SUB, sub, 0)

        def scatter(g, _):
            for j in range(UNROLL):
                e = base + g * UNROLL + j
                at, to = row(src[e]), row(rel[e])
                gleft[at, :] = gleft[at, :] + a_st[spot(g, j), :]
                grel[to, :] = grel[to, :] + r_st[spot(g, j), :]
            return 0

        lax.fori_loop(0, groups, scatter, 0)
        return 0

    lax.fori_loop(0, (live + TILE - 1) // TILE, tile, 0)

    @pl.when(c == SPANS - 1)
    def _():
        rel_out[...] = grel[...].astype(BF16)
        adagrad_tables(gleft, left_t, state, new_ref, new_state)


def left_update(src, rel, live, source, relation, grad_product, left_t, state):
    smem = pl.BlockSpec(memory_space=pltpu.SMEM)
    vmem = pl.BlockSpec(memory_space=pltpu.VMEM)
    block = pl.BlockSpec((1, SPAN_PAD, 512), lambda c: (c, 0, 0))
    return pl.pallas_call(
        left_kernel,
        grid=(SPANS,),
        out_shape=[
            jax.ShapeDtypeStruct((WIDTH, ROWS), F32),
            jax.ShapeDtypeStruct((1, ROWS), F32),
            jax.ShapeDtypeStruct((REL_TALL, 128), BF16),
        ],
        in_specs=[smem] * 3 + [block] * 3 + [vmem] * 2,
        out_specs=[vmem] * 3,
        scratch_shapes=[pltpu.VMEM((4 * ROWS, 128), F32), pltpu.VMEM((REL_TALL, 128), F32)]
        + [pltpu.VMEM((4 * TILE, 128), F32)] * 2,
        compiler_params=pltpu.CompilerParams(**PARAMS),
        cost_estimate=pl.CostEstimate(flops=0, bytes_accessed=240_000_000, transcendentals=0),
        name="left_update",
    )(src, rel, live, source, relation, grad_product, left_t, state)


def right_kernel(ids, *refs):
    backs = refs[:PARTS]
    g_hbm, right_t, state, new_ref, new_state, total, stage, sem = refs[PARTS:]
    c = pl.program_id(0)

    @pl.when(c == 0)
    def _():
        copy = pltpu.make_async_copy(g_hbm, total.at[pl.ds(0, 4 * ROWS)], sem)
        copy.start()
        copy.wait()

    def peer(back_ref, p, _):
        parts = unpack_wire(back_ref[p].astype(F32))
        stage[...] = jnp.stack(
            [part.reshape(SLOT // 8, 8, 128) for part in parts], 1
        ).reshape(4 * SLOT, 128)
        base = p * (SPANS * SLOT) + c * SLOT

        def scatter(g, _):
            for j in range(UNROLL):
                at = row(ids[base + g * UNROLL + j])
                total[at, :] = total[at, :] + stage[spot(g, j), :]
            return 0

        lax.fori_loop(0, SLOT // UNROLL, scatter, 0)
        return 0

    for k, back_ref in enumerate(backs):

        @pl.when(c // PART == k)
        def _():
            lax.fori_loop(0, PEERS, functools.partial(peer, back_ref), 0)

    @pl.when(c == SPANS - 1)
    def _():
        adagrad_tables(total, right_t, state, new_ref, new_state)


def right_update(ids, backs, grad, right_t, state):
    def part(k):
        return pl.BlockSpec(
            (PEERS, WIRE, 128), lambda c: (0, jnp.clip(c - k * PART, 0, PART - 1), 0)
        )

    vmem = pl.BlockSpec(memory_space=pltpu.VMEM)
    return pl.pallas_call(
        right_kernel,
        grid=(SPANS,),
        out_shape=[
            jax.ShapeDtypeStruct((WIDTH, ROWS), F32),
            jax.ShapeDtypeStruct((1, ROWS), F32),
        ],
        in_specs=[
            pl.BlockSpec(memory_space=pltpu.SMEM),
            *(part(k) for k in range(PARTS)),
            pl.BlockSpec(memory_space=pl.ANY),
            vmem,
            vmem,
        ],
        out_specs=[vmem] * 2,
        scratch_shapes=[
            pltpu.VMEM((TALL, 128), F32),
            pltpu.VMEM((4 * SLOT, 128), F32),
            pltpu.SemaphoreType.DMA,
        ],
        compiler_params=pltpu.CompilerParams(**PARAMS),
        cost_estimate=pl.CostEstimate(flops=0, bytes_accessed=160_000_000, transcendentals=0),
        name="right_update",
    )(ids, *backs, grad, right_t, state)


def places():
    grp, shard = lax.axis_index("grp"), lax.axis_index("shard")
    core, chip = lax.rem(grp, CORES), lax.div(grp, CORES)

    def other_core():
        return (chip * CORES + 1 - core, shard)

    def along_grp(d):
        return (lax.rem(chip + d, CHIPS) * CORES + core, shard)

    def along_shard(d):
        return (grp, lax.rem(shard + d, PEERS))

    return core, chip, shard, other_core, along_grp, along_shard


def greet(devices):
    barrier = pltpu.get_barrier_semaphore()
    for device in devices:
        pl.semaphore_signal(
            barrier, inc=1, device_id=device, device_id_type=pl.DeviceIdType.MESH
        )
    pl.semaphore_wait(barrier, len(devices))


def sender(sends, recvs):
    def send(src, dst, slot, to):
        copy = pltpu.make_async_remote_copy(
            src_ref=src, dst_ref=dst, send_sem=sends.at[slot], recv_sem=recvs.at[slot],
            device_id=to, device_id_type=pl.DeviceIdType.MESH,
        )
        copy.start()
        return copy

    return send


def relation_sum_kernel(mine, out, got_0, half, got_1, sum_1, got_2, sum_2, sends, recvs):
    core, chip, shard, other_core, along_grp, along_shard = places()
    steps = range(1, PEERS)
    greet(
        [other_core()] + [along_shard(d) for d in steps] + [along_grp(d) for d in steps]
    )
    send = sender(sends, recvs)
    copy = send(mine.at[1 - core], got_0, 0, other_core())
    copy.wait()

    def add(p, _):
        half[p] = (mine[core, p].astype(F32) + got_0[p].astype(F32)).astype(BF16)
        return 0

    lax.fori_loop(0, PEERS, add, 0)
    copies = [
        send(half.at[lax.rem(shard + d, PEERS)], got_1.at[d - 1], d, along_shard(d))
        for d in steps
    ]
    for copy in copies:
        copy.wait()

    def total_of(k, _):
        total = mine[core, shard, k].astype(F32) + got_0[shard, k].astype(F32)
        for d in range(PEERS - 1):
            total = total + got_1[d, k].astype(F32)
        sum_1[k] = total
        return 0

    lax.fori_loop(0, CHIPS, total_of, 0)
    copies = [
        send(sum_1.at[lax.rem(chip + d, CHIPS)], got_2.at[d - 1], 7 + d, along_grp(d))
        for d in steps
    ]
    for copy in copies:
        copy.wait()
    total = sum_1[chip]
    for d in range(CHIPS - 1):
        total = total + got_2[d]
    sum_2[...] = total
    out[chip] = total
    copies = [send(sum_2, out.at[chip], 14 + d, along_grp(d)) for d in steps]
    for copy in copies:
        copy.wait()


def relation_sum(grad):
    vmem = pl.BlockSpec(memory_space=pltpu.VMEM)
    return pl.pallas_call(
        relation_sum_kernel,
        out_shape=jax.ShapeDtypeStruct((CHIPS, REL_SHARE, 128), F32),
        in_specs=[vmem],
        out_specs=vmem,
        scratch_shapes=[
            pltpu.VMEM((PEERS, CHIPS, REL_SHARE, 128), BF16),
            pltpu.VMEM((PEERS, CHIPS, REL_SHARE, 128), BF16),
            pltpu.VMEM((PEERS - 1, CHIPS, REL_SHARE, 128), BF16),
            pltpu.VMEM((CHIPS, REL_SHARE, 128), F32),
            pltpu.VMEM((CHIPS - 1, REL_SHARE, 128), F32),
            pltpu.VMEM((REL_SHARE, 128), F32),
            pltpu.SemaphoreType.DMA((22,)),
            pltpu.SemaphoreType.DMA((22,)),
        ],
        compiler_params=pltpu.CompilerParams(
            collective_id=0, has_side_effects=True, vmem_limit_bytes=32 * 1024 * 1024
        ),
        cost_estimate=pl.CostEstimate(flops=0, bytes_accessed=4_000_000, transcendentals=0),
        name="relation_sum",
    )(grad.reshape(CORES, PEERS, CHIPS, REL_SHARE, 128))


def relation_spread_kernel(mine, out, sends, recvs):
    core, chip, shard, other_core, along_grp, along_shard = places()
    steps = range(1, PEERS)
    greet([other_core()] + [along_shard(d) for d in steps])
    send = sender(sends, recvs)
    copies = [send(mine, out.at[core, shard], d, along_shard(d)) for d in steps]
    out[core, shard] = mine[...]
    across = [send(mine, out.at[core, shard], 8, other_core())]
    for d in steps:
        copies[d - 1].wait_recv()
        block = out.at[core, lax.rem(shard + PEERS - d, PEERS)]
        across.append(send(block, block, 8 + d, other_core()))
    for copy in copies:
        copy.wait_send()
    for copy in across:
        copy.wait()


def relation_spread(total):
    vmem = pl.BlockSpec(memory_space=pltpu.VMEM)
    out = pl.pallas_call(
        relation_spread_kernel,
        out_shape=jax.ShapeDtypeStruct((CORES, PEERS, CHIPS, REL_SHARE, 128), F32),
        in_specs=[vmem],
        out_specs=vmem,
        scratch_shapes=[pltpu.SemaphoreType.DMA((16,)), pltpu.SemaphoreType.DMA((16,))],
        compiler_params=pltpu.CompilerParams(
            collective_id=1, has_side_effects=True, vmem_limit_bytes=32 * 1024 * 1024
        ),
        cost_estimate=pl.CostEstimate(flops=0, bytes_accessed=4_000_000, transcendentals=0),
        name="relation_spread",
    )(total)
    return out.reshape(REL_TALL, 128)


def relation_kernel(g_ref, rel_t, state, new_ref, new_state):
    for i in range(RELS_PAD // 128):
        low, high = i * 128, min(RELS, i * 128 + 128)
        new, ns = adagrad_block(g_ref, rel_t[:, low : low + 128], state[:, low : low + 128], i)
        new_ref[:, low:high] = new[:, : high - low]
        new_state[:, low:high] = ns[:, : high - low]


def relation_update(grad, rel_t, state):
    vmem = pl.BlockSpec(memory_space=pltpu.VMEM)
    return pl.pallas_call(
        relation_kernel,
        out_shape=[
            jax.ShapeDtypeStruct((WIDTH, RELS), F32),
            jax.ShapeDtypeStruct((1, RELS), F32),
        ],
        in_specs=[vmem] * 3,
        out_specs=[vmem] * 2,
        compiler_params=pltpu.CompilerParams(**PARAMS),
        name="relation_update",
    )(grad, rel_t, state)


def passed_along(block, axis, distance):
    devices = range(lax.axis_size(axis))
    route = [((i - distance) % len(devices), i) for i in devices]
    return lax.ppermute(block, axis, route)


def exchange(x):
    return lax.all_to_all(x, "shard", split_axis=0, concat_axis=0, tiled=True)


def local(
    left_table, right_table, left_state, right_state, relations, relation_state,
    source_rows, relation_ids, target_rows, negative_rows, span_sizes,
):
    left_t, right_t = left_table.T, right_table.T
    wanted = negative_rows.reshape(SPANS, PEERS, NEG_PER).transpose(1, 0, 2)
    wanted = jnp.pad(wanted, ((0, 0), (0, 0), (0, SLOT - NEG_PER)), constant_values=DUMP)
    asked = exchange(wanted.reshape(PEERS, SPANS * SLOT)).reshape(-1)
    served = serve(asked, right_t)
    got = exchange(served)

    def flat(ids):
        return jnp.pad(ids, ((0, 0), (0, SPAN_PAD - ids.shape[1]))).reshape(-1)

    src, rel, tgt = flat(source_rows), flat(relation_ids), flat(target_rows)
    live = span_sizes.reshape(SPANS)
    rel_t = jnp.pad(relations.T, ((0, 0), (0, RELS_PAD - RELS)))
    rel_state = jnp.pad(relation_state, (0, RELS_PAD - RELS), constant_values=1.0)
    source, relation, product, pos_target, grad_right = forward(
        src, rel, tgt, live, left_t, right_t, rel_t
    )
    grad_product, returned = None, []
    for k in range(PARTS):
        grad_product, back = negatives(live, product, pos_target, got, k * PART, grad_product)
        returned.append(exchange(back))
    new_left, new_left_state, grad_rel = left_update(
        src, rel, live, source, relation, grad_product, left_t, left_state.reshape(1, ROWS)
    )
    rel_share = relation_sum(grad_rel)
    sent_left, returned, rel_share = lax.optimization_barrier(
        (new_left.astype(jnp.float16), returned, rel_share)
    )
    moved_left = passed_along(sent_left, "grp", ROUND)
    new_right, new_right_state = right_update(
        asked, returned, grad_right, right_t, right_state.reshape(1, ROWS)
    )
    rel_share, sent = lax.optimization_barrier((rel_share, new_right.astype(jnp.float16)))
    rel_total = relation_spread(rel_share)
    moved_right = passed_along(sent, "grp", ROUND)
    states = jnp.concatenate([new_left_state, new_right_state], 0)
    moved_states = passed_along(states, "grp", ROUND)
    new_rel, new_rel_state = relation_update(rel_total, rel_t, rel_state.reshape(1, RELS_PAD))
    new_rel, moved_left, moved_states = lax.optimization_barrier(
        (new_rel, moved_left, moved_states)
    )
    return (
        moved_left.astype(F32).T,
        moved_states[0],
        moved_right.astype(F32).T,
        moved_states[1],
        new_rel.T,
        new_rel_state.reshape(RELS),
    )


def solution(mesh):
    rows, flat = P(("grp", "shard"), None), P(("grp", "shard"))
    return jax.shard_map(
        local,
        mesh=mesh,
        in_specs=(rows, rows, flat, flat, P(), P(), rows, rows, rows, rows, rows),
        out_specs=(rows, flat, rows, flat, P(), P()),
        check_vma=False,
    )
```

time: 1720 us -> 470 us (0.27); the launches traced: 1700 us -> 470 us
  local copies, waits for them, and re-layouts: 679 us -> 7.31 us
  other arithmetic: 530 us -> 20.4 us
  Pallas kernels: 0 us -> 383 us
  waiting for transfers between devices: 333 us -> 25.4 us
  matrix products: 97.1 us -> 0 us
    scatter-add x28 -> x0, other arithmetic: 384 us -> none  [the longest x9 124 us: step(): grad_right = grad_right.at[targets].add(grad_target)]
    pallas_call x0 -> x8, Pallas kernels: none -> 383 us  [the longest x1 88.6 us: forward(): pl.pallas_call(forward_kernel, grid=(SPANS,), out_shape=[per_edge] * 4 +...]
    gather x38 -> x0, local copies, waits for them, and re-layouts: 285 us -> none  [the longest x18 103 us: step(): target = right_table[targets]]
    all_to_all x3 -> x2, waiting for transfers between devices: 124 us -> 0.01 us  [exchange(): return lax.all_to_all(x, 'shard', split_axis=0, concat_axis=0, tiled=True)]
    ppermute x4 -> x3, waiting for transfers between devices: 145 us -> 25.4 us  [passed_along(): return lax.ppermute(block, axis, route)]
    dot_general x27 -> x0, matrix products: 97.1 us -> none  [the longest x9 35.6 us: span_terms(): lax.dot_general(neg_grad, product_b, (((0,), (0,)), ((), ())), preferred_...]
    while x199 -> x0, local copies, waits for them, and re-layouts: 91.5 us -> none
    psum x1 -> x0, waiting for transfers between devices: 64.5 us -> none  [local(): rel_total = lax.psum(grad_rel, ('grp', 'shard'))]
  transfers between devices with their start and end apart: 8 -> 5, of which waited for: 5 -> 1; matrix products, arithmetic and copies ran while one was open for 9% -> 4% of each run, Pallas kernels for 0% -> 63%
where the time goes in v1:
time: 470 us
  Pallas kernels  383 us (81%)
  waiting for transfers between devices  25.4 us (5%)
  starting transfers between devices  20.7 us (4%)
  other arithmetic  20.4 us (4%)
  blocking collectives  11.8 us (3%)
  local copies, waits for them, and re-layouts  7.31 us (2%)
    pallas_call x1, Pallas kernels, forward(): pl.pallas_call(forward_kernel, grid=(SPANS,), out_shape=[per_edge] * 4 +...  88.6 us
    pallas_call x1, Pallas kernels, relation_sum(): pl.pallas_call(relation_sum_kernel, out_shape=jax.ShapeDtypeStruct((CHIPS...  54.2 us
    pallas_call x1, Pallas kernels, negatives(): pl.pallas_call(functools.partial(negatives_kernel, first), grid=(PART,),...  53.2 us
    pallas_call x1, Pallas kernels, relation_spread(): pl.pallas_call(relation_spread_kernel, out_shape=jax.ShapeDtypeStruct((CO...  50.4 us
    pallas_call x1, Pallas kernels, left_update(): pl.pallas_call(left_kernel, grid=(SPANS,), out_shape=[jax.ShapeDtypeStruc...  49.5 us
    pallas_call x1, Pallas kernels, right_update(): pl.pallas_call(right_kernel, grid=(SPANS,), out_shape=[jax.ShapeDtypeStru...  49.1 us
    pallas_call x1, Pallas kernels, serve(): pl.pallas_call(serve_kernel, grid=(PEERS,), out_shape=jax.ShapeDtypeStruc...  33.6 us
    ppermute x3, waiting for transfers between devices, passed_along(): return lax.ppermute(block, axis, route)  25.4 us
  transfers between devices with their start and end apart: 5, of which 1 were waited for; matrix products, arithmetic and copies ran while one was open for 4% of the time, Pallas kernels for 63%

profile of v1, /device:TPU:1, one launch (start us, length us, event | category | flops | bytes accessed | tf_op | source)
XLA Modules:
  0.0 469.9 jit_solution(3777811918573038765)
XLA Ops:
  0.6 0.9 reshape.57
  1.6 11.8 %all_to_all.19 = s32[8,1,1152]{2,1,0:T(1,128)} all-to-all(s32[8,1,1152]{2,1,0:T(1,128)S(1)} %copy.17), channel_id=1, replica_groups=mesh['grp'=16,'shard'=8] {'shard'}, dimensions={0} | all-to-all | bytes 73728 | tf_op jit(solution)/shard_map/all_to_all | solution.py:658
  13.4 33.6 %serve.1 = bf16[8,3600,128]{2,1,0:T(8,128)(2,1)} custom-call(s32[9216]{0:T(1024)} %bitcast.27, f32[400,4096]{1,0:T(8,128)} %bitcast.21), custom_call_target="tpu_custom_call" | custom-call | bytes 80000000 | tf_op jit(solution)/shard_map/serve/pallas_call | solution.py:129
  47.1 0.0 copy-start.3
  47.1 0.0 copy-start.4
  47.1 0.0 copy-start.5
  47.1 0.0 copy-start.2
  47.1 5.0 %all-to-all-start.1 = ((bf16[8,3600,128]{2,1,0:T(8,128)(2,1)}), bf16[8,3600,128]{2,1,0:T(8,128)(2,1)}, u32[]{:S(2)}, u32[]{:S(2)}) async-start(bf16[8,3600,128]{2,1,0:T(8,128)(2,1)} %serve.1), calls=%async_computation.1 | async-start | bytes 14745600 | tf_op jit(solution)/shard_map/all_to_all | solution.py:658
  52.0 0.0 copy-done.3
  52.1 0.6 reshape.53.src
  52.7 0.0 copy-done.4
  52.7 0.6 reshape.54.rel
  53.3 0.0 copy-done.5
  53.3 0.6 reshape.56.tgt
  54.0 0.0 copy-done.2
  54.0 1.5 pad.25.rel_t
  55.5 88.6 %forward.1 = (bf16[9,1024,512]{2,1,0:T(8,128)(2,1)}, bf16[9,1024,512]{2,1,0:T(8,128)(2,1)}, bf16[9,1024,512]{2,1,0:T(8,128)(2,1)}, bf16[9,1024,512]{2,1,0:T(8,128)(2,1)}, f32[16384,128]{1,0:T(8,128)}) custom-call(s32[9216]{0:T(1024)} %reshape.53.src, s32[9216]{0:T(1024)} %reshape.54.rel, s32[9216]{0:T(1024)} %reshape.56.tgt, s32[9]{0:T(128)} %bitcast.34, ...), custom_call_target="tpu_custom_call" | custom-call | bytes 280000000 | tf_op jit(solution)/shard_map/forward/pallas_call | solution.py:237
  144.1 0.0 all-to-all-done.1.got_ref
  144.1 53.2 %negatives.1 = (bf16[9,1024,512]{2,1,0:T(8,128)(2,1)}, bf16[8,3600,128]{2,1,0:T(8,128)(2,1)}) custom-call(s32[9]{0:T(128)} %bitcast.35, bf16[9,1024,512]{2,1,0:T(8,128)(2,1)} %get-tuple-element.30.p_ref, bf16[9,1024,512]{2,1,0:T(8,128)(2,1)} %get-tuple-element.31.pt_ref, bf16[8,3600,128]{2,1,0:T(8,128)(2,1)} %all-to-all-done.1.got_ref), custom_call_target="tpu_custom_call" | custom-call | flops 14000000000 | bytes 60000000 | tf_op jit(solution)/shard_map/negatives/pallas_call | solution.py:317
  197.3 8.2 %all-to-all-start.2 = ((bf16[8,3600,128]{2,1,0:T(8,128)(2,1)}), bf16[8,3600,128]{2,1,0:T(8,128)(2,1)}, u32[]{:S(2)}, u32[]{:S(2)}) async-start(bf16[8,3600,128]{2,1,0:T(8,128)(2,1)} %get-tuple-element.34), calls=%async_computation.2 | async-start | bytes 14745600 | tf_op jit(solution)/shard_map/all_to_all | solution.py:658
  205.5 49.5 %left_update.1 = (f32[400,4096]{1,0:T(8,128)}, f32[1,4096]{1,0:T(1,128)}, bf16[6144,128]{1,0:T(8,128)(2,1)}) custom-call(s32[9216]{0:T(1024)} %reshape.53.src, s32[9216]{0:T(1024)} %reshape.54.rel, s32[9]{0:T(128)} %bitcast.36, bf16[9,1024,512]{2,1,0:T(8,128)(2,1)} %get-tuple-element.28.s_ref, bf16[9,1024,512]{2,1,0:T(8,128)(2,1)} %get-tuple-element.29.b_ref, ...), custom_call_target="tpu_custom_call" | custom-call | bytes 240000000 | tf_op jit(solution)/shard_map/left_update/pallas_call | solution.py:396
  255.0 0.0 copy-start.1
  255.0 3.5 convert_element_type.10
  258.5 0.0 copy-done.1
  258.5 54.2 %relation_sum.1.mine = f32[8,48,128]{2,1,0:T(8,128)S(1)} custom-call(bf16[2,8,8,48,128]{4,3,2,1,0:T(8,128)(2,1)S(1)} %bitcast.20), custom_call_target="tpu_custom_call" | custom-call | bytes 4000000 | tf_op jit(solution)/shard_map/relation_sum/pallas_call | solution.py:570
  312.7 0.0 all-to-all-done.2.refs_0_
  312.7 3.5 collective-permute-start
  316.1 49.1 %right_update.1 = (f32[400,4096]{1,0:T(8,128)}, f32[1,4096]{1,0:T(1,128)}) custom-call(s32[9216]{0:T(1024)} %bitcast.28, bf16[8,3600,128]{2,1,0:T(8,128)(2,1)} %all-to-all-done.2.refs_0_, f32[16384,128]{1,0:T(8,128)} %get-tuple-element.38.refs_1_, f32[400,4096]{1,0:T(8,128)} %bitcast.23, f32[1,4096]{1,0:T(1,128)} %bitcast.33), custom_call_target="tpu_custom_call" | custom-call | bytes 160000000 | tf_op jit(solution)/shard_map/right_update/pallas_call | solution.py:459
  365.2 0.0 copy-start.6
  365.2 0.0 copy-start.7
  365.3 0.0 copy-start.8
  365.3 5.0 %convert_element_type.11 = f16[400,4096]{1,0:T(8,128)(2,1)} convert(f32[400,4096]{1,0:T(8,128)} %get-tuple-element.39) | non-fusion elementwise | flops 1638400 | bytes 9830400 | tf_op jit(solution)/shard_map/convert_element_type | solution.py:697
  370.3 0.0 collective-permute-start.2
  370.3 0.0 copy-done.6
  370.4 0.0 copy-done.7
  370.4 4.0 collective-permute-start.1
  374.4 0.0 copy-done.8
  374.4 0.6 reshape.63.state
  375.0 50.4 %relation_spread.1 = f32[2,8,8,48,128]{4,3,2,1,0:T(8,128)S(1)} custom-call(f32[8,48,128]{2,1,0:T(8,128)S(1)} %relation_sum.1.mine), custom_call_target="tpu_custom_call" | custom-call | bytes 4000000 | tf_op jit(solution)/shard_map/relation_spread/pallas_call | solution.py:613
  425.4 0.0 copy-start
  425.4 1.7 copy-done
  427.1 4.9 %relation_update.1 = (f32[400,1345]{1,0:T(8,128)}, f32[1,1345]{1,0:T(1,128)}) custom-call(f32[6144,128]{1,0:T(8,128)} %bitcast.19, f32[400,1408]{1,0:T(8,128)} %pad.25.rel_t, f32[1,1408]{1,0:T(1,128)} %reshape.63.state), custom_call_target="tpu_custom_call" | custom-call | tf_op jit(solution)/shard_map/relation_update/pallas_call | solution.py:638
  432.0 1.3 reduce
  433.3 25.4 %collective-permute-done.1 = f32[2,4096]{1,0:T(2,128)S(1)} collective-permute-done((f32[2,4096]{1,0:T(2,128)S(1)}, f32[2,4096]{1,0:T(2,128)S(1)}, u32[]{:S(2)}, u32[]{:S(2)}) %collective-permute-start.1) | collective-permute-done | bytes 32800 | tf_op jit(solution)/shard_map/ppermute | solution.py:654
  458.7 0.0 collective-permute-done
  458.7 0.6 fusion
  459.4 5.3 %convert_bitcast_fusion.1 = f32[4096,400]{0,1:T(8,128)} fusion(f16[400,4096]{1,0:T(8,128)(2,1)} %collective-permute-done), kind=kLoop, calls=%fused_computation.1 | loop fusion | flops 1638400 | bytes 9830400 | tf_op jit(solution)/shard_map/transpose | solution.py:707
  464.6 0.0 collective-permute-done.2
  464.6 5.3 %convert_bitcast_fusion = f32[4096,400]{0,1:T(8,128)} fusion(f16[400,4096]{1,0:T(8,128)(2,1)} %collective-permute-done.2), kind=kLoop, calls=%fused_computation | loop fusion | flops 1638400 | bytes 9830400 | tf_op jit(solution)/shard_map/transpose | solution.py:709
  (7 shorter events, 0.1 us)
Async XLA Ops:
  47.1 5.0 %copy-start.3 = (s32[9,1000]{1,0:T(8,128)S(1)}, s32[9,1000]{1,0:T(8,128)}, u32[]{:S(2)}) copy-start(s32[9,1000]{1,0:T(8,128)} %param.17) | copy-start | bytes 108004
  47.1 5.6 %copy-start.4 = (s32[9,1000]{1,0:T(8,128)S(1)}, s32[9,1000]{1,0:T(8,128)}, u32[]{:S(2)}) copy-start(s32[9,1000]{1,0:T(8,128)} %param.18) | copy-start | bytes 108004
  47.1 6.3 %copy-start.5 = (s32[9,1000]{1,0:T(8,128)S(1)}, s32[9,1000]{1,0:T(8,128)}, u32[]{:S(2)}) copy-start(s32[9,1000]{1,0:T(8,128)} %param.19) | copy-start | bytes 108004
  47.1 6.9 %copy-start.2 = (f32[1345,400]{0,1:T(8,128)S(1)}, f32[1345,400]{0,1:T(8,128)}, u32[]{:S(2)}) copy-start(f32[1345,400]{0,1:T(8,128)} %param.15) | copy-start | bytes 6456004
  47.1 97.1 %all-to-all-start.1 = ((bf16[8,3600,128]{2,1,0:T(8,128)(2,1)}), bf16[8,3600,128]{2,1,0:T(8,128)(2,1)}, u32[]{:S(2)}, u32[]{:S(2)}) async-start(bf16[8,3600,128]{2,1,0:T(8,128)(2,1)} %serve.1), calls=%async_computation.1 | async-start | bytes 14745600 | tf_op jit(solution)/shard_map/all_to_all | solution.py:658
  197.3 115.3 %all-to-all-start.2 = ((bf16[8,3600,128]{2,1,0:T(8,128)(2,1)}), bf16[8,3600,128]{2,1,0:T(8,128)(2,1)}, u32[]{:S(2)}, u32[]{:S(2)}) async-start(bf16[8,3600,128]{2,1,0:T(8,128)(2,1)} %get-tuple-element.34), calls=%async_computation.2 | async-start | bytes 14745600 | tf_op jit(solution)/shard_map/all_to_all | solution.py:658
  255.0 3.5 copy-start.1
  312.7 146.0 %collective-permute-start = (f16[400,4096]{1,0:T(8,128)(2,1)S(1)}, f16[400,4096]{1,0:T(8,128)(2,1)}, u32[]{:S(2)}, u32[]{:S(2)}) collective-permute-start(f16[400,4096]{1,0:T(8,128)(2,1)S(1)} %convert_element_type.10), channel_id=1, source_target_pairs={{88,0},{96,8},{104,16},{112,24},{120,32},{0,40},{8,48},{16,56},{24... | collective-permute-start | bytes 9830408 | tf_op jit(solution)/shard_map/ppermute | solution.py:654
  365.2 5.1 %copy-start.6 = (f32[1,4096]{1,0:T(1,128)S(1)}, f32[1,4096]{1,0:T(1,128)}, u32[]{:S(2)}) copy-start(f32[1,4096]{1,0:T(1,128)} %get-tuple-element.43) | copy-start | bytes 49156
  365.2 5.1 %copy-start.7 = (f32[1,4096]{1,0:T(1,128)S(1)}, f32[1,4096]{1,0:T(1,128)}, u32[]{:S(2)}) copy-start(f32[1,4096]{1,0:T(1,128)} %get-tuple-element.44) | copy-start | bytes 49156
  365.3 9.2 %copy-start.8 = (f32[1345]{0:T(1024)S(1)}, f32[1345]{0:T(1024)}, u32[]{:S(2)}) copy-start(f32[1345]{0:T(1024)} %param.16) | copy-start | bytes 16144
  370.3 94.3 %collective-permute-start.2 = (f16[400,4096]{1,0:T(8,128)(2,1)}, f16[400,4096]{1,0:T(8,128)(2,1)}, u32[]{:S(2)}, u32[]{:S(2)}) collective-permute-start(f16[400,4096]{1,0:T(8,128)(2,1)} %convert_element_type.11), channel_id=1, source_target_pairs={{88,0},{96,8},{104,16},{112,24},{120,32},{0,40},{8,48},{16,56},{24... | collective-permute-start | bytes 9830408 | tf_op jit(solution)/shard_map/ppermute | solution.py:654
  370.4 88.3 %collective-permute-start.1 = (f32[2,4096]{1,0:T(2,128)S(1)}, f32[2,4096]{1,0:T(2,128)S(1)}, u32[]{:S(2)}, u32[]{:S(2)}) collective-permute-start(f32[2,4096]{1,0:T(2,128)S(1)} %pad_maximum_fusion), channel_id=1, source_target_pairs={{88,0},{96,8},{104,16},{112,24},{120,32},{0,40},{8,48},{16,56},{24... | collective-permute-start | bytes 98312 | tf_op jit(solution)/shard_map/ppermute | solution.py:654
  425.4 1.7 copy-start

commit v2 on v1

--- a/solution.py
+++ b/solution.py
@@ -55,7 +55,7 @@
             out_ref[pl.ds(i * 512 + c, 128, stride=4), :] = part.T
         return 0
 
-    lax.fori_loop(0, count // 128, block, 0)
+    lax.fori_loop(0, count // 128, block, 0, unroll=8 if count == ROWS else 1)
 
 
 def adagrad_block(g_ref, t, state, i):
@@ -77,15 +77,40 @@
         new_state_ref[:, at] = state
         return 0
 
-    lax.fori_loop(0, ROWS // 128, block, 0)
+    lax.fori_loop(0, ROWS // 128, block, 0, unroll=2)
 
 
 def spot(group, j):
-    return pl.ds(group * (4 * UNROLL) + (j // 8) * 32 + (j % 8), 4, stride=8)
+    return pl.ds(group * (4 * UNROLL) + 4 * j, 4)
+
+
+def chunk(first, count, c):
+    return pl.ds(first * 4 + c, count, stride=4)
 
 
 def row(index):
     return pl.ds(pl.multiple_of(index * 4, 4), 4)
+
+
+TOGETHER = 1
+
+
+def add_rows(*work):
+    for first in range(0, len(work[0][1]), TOGETHER):
+        for ref, indices, values in work:
+            ids = indices[first : first + TOGETHER]
+            adds = [value() for value in values[first : first + TOGETHER]]
+            new = [ref[row(i), :] + add for i, add in zip(ids, adds)]
+            for k in range(len(ids)):
+                for j in range(k):
+                    same = jnp.where(ids[j] == ids[k], 1.0, 0.0)
+                    new[k] = new[k] + same * adds[j]
+            for i, value in zip(ids, new):
+                ref[row(i), :] = value
+
+
+def staged(stage, group):
+    return [functools.partial(lambda j: stage[spot(group, j), :], j) for j in range(UNROLL)]
 
 
 def serve_kernel(ids, t_ref, out_ref, table, stage):
@@ -106,9 +131,8 @@
                 stage[spot(g, j), :] = table[row(ids[base + g * UNROLL + j]), :]
             return 0
 
-        lax.fori_loop(0, SLOT // UNROLL, group, 0)
-        s = stage[...].reshape(SLOT // 8, 4, 8, 128)
-        re0, re1, im0, im1 = (s[:, k].reshape(SLOT, 128) for k in range(4))
+        lax.fori_loop(0, SLOT // UNROLL, group, 0, unroll=8)
+        re0, re1, im0, im1 = (stage[chunk(0, SLOT, k), :] for k in range(4))
         moved = pltpu.roll(im1, REST, 1)
         mixed = jnp.where(lanes < REST, re1, moved)
         tail = jnp.where(lanes < 16, moved, 0.0)
@@ -188,38 +212,34 @@
         lax.fori_loop(0, groups, gather, 0)
 
         def sub(k, _):
-            at = pl.ds(pl.multiple_of(k * (4 * SUB), 4 * SUB), 4 * SUB)
-            s, b, q = (st[at, :].reshape(SUB // 8, 4, 8, 128) for st in (s_st, b_st, t_st))
-            re = [s[:, i] * b[:, i] - s[:, i + 2] * b[:, i + 2] for i in range(2)]
-            im = [s[:, i] * b[:, i + 2] + s[:, i + 2] * b[:, i] for i in range(2)]
+            s, b, q = (
+                [st[chunk(k * SUB, SUB, i), :] for i in range(4)] for st in (s_st, b_st, t_st)
+            )
+            re = [s[i] * b[i] - s[i + 2] * b[i + 2] for i in range(2)]
+            im = [s[i] * b[i + 2] + s[i + 2] * b[i] for i in range(2)]
             prod = re + im
             positive = jnp.sum(
-                prod[0] * q[:, 0] + prod[1] * q[:, 1] + prod[2] * q[:, 2] + prod[3] * q[:, 3],
+                prod[0] * q[0] + prod[1] * q[1] + prod[2] * q[2] + prod[3] * q[3],
                 -1, keepdims=True,
             )
-            shape = (SUB // 8, 8, 1)
-            where = (
-                k * SUB
-                + lax.broadcasted_iota(jnp.int32, shape, 0) * 8
-                + lax.broadcasted_iota(jnp.int32, shape, 1)
-            )
+            where = k * SUB + lax.broadcasted_iota(jnp.int32, (SUB, 1), 0)
             pos_grad = jnp.where(where < left_over, -jax.nn.sigmoid(-positive), 0.0)
-            g_st[at, :] = jnp.stack([pos_grad * x for x in prod], 1).reshape(4 * SUB, 128)
+            for i in range(4):
+                g_st[chunk(k * SUB, SUB, i), :] = pos_grad * prod[i]
             rows = pl.ds(pl.multiple_of(t * TILE + k * SUB, SUB), SUB)
             for i in range(4):
                 lanes = slice(i * 128, i * 128 + 128)
-                s_out[0, rows, lanes] = s[:, i].reshape(SUB, 128).astype(BF16)
-                b_out[0, rows, lanes] = b[:, i].reshape(SUB, 128).astype(BF16)
-                p_out[0, rows, lanes] = prod[i].reshape(SUB, 128).astype(BF16)
-                pt_out[0, rows, lanes] = (pos_grad * q[:, i]).reshape(SUB, 128).astype(BF16)
+                s_out[0, rows, lanes] = s[i].astype(BF16)
+                b_out[0, rows, lanes] = b[i].astype(BF16)
+                p_out[0, rows, lanes] = prod[i].astype(BF16)
+                pt_out[0, rows, lanes] = (pos_grad * q[i]).astype(BF16)
             return 0
 
-        lax.fori_loop(0, TILE // SUB, sub, 0)
+        lax.fori_loop(0, TILE // SUB, sub, 0, unroll=8)
 
         def scatter(g, _):
-            for j in range(UNROLL):
-                at = row(tgt[base + g * UNROLL + j])
-                g_ref[at, :] = g_ref[at, :] + g_st[spot(g, j), :]
+            ids = [tgt[base + g * UNROLL + j] for j in range(UNROLL)]
+            add_rows((g_ref, ids, staged(g_st, g)))
             return 0
 
         lax.fori_loop(0, groups, scatter, 0)
@@ -264,7 +284,7 @@
             neg[at, k * 128 : k * 128 + 128] = part.astype(BF16)
         return 0
 
-    lax.fori_loop(0, PEERS, unpack, 0)
+    lax.fori_loop(0, PEERS, unpack, 0, unroll=4)
     acc[...] = jnp.zeros_like(acc)
 
     def tile(t, _):
@@ -301,7 +321,7 @@
         back_ref[p, 384:400, :] = packed.astype(BF16)
         return 0
 
-    lax.fori_loop(0, PEERS, pack, 0)
+    lax.fori_loop(0, PEERS, pack, 0, unroll=4)
 
 
 def negatives(live, product, pos_target, got, first, grad_product):
@@ -355,27 +375,22 @@
         def sub(k, _):
             rows = pl.ds(pl.multiple_of(t * TILE + k * SUB, SUB), SUB)
             s, b, g = (
-                [
-                    ref[0, rows, i * 128 : i * 128 + 128].astype(F32).reshape(SUB // 8, 8, 128)
-                    for i in range(4)
-                ]
+                [ref[0, rows, i * 128 : i * 128 + 128].astype(F32) for i in range(4)]
                 for ref in (s_ref, b_ref, gp_ref)
             )
-            at = pl.ds(pl.multiple_of(k * (4 * SUB), 4 * SUB), 4 * SUB)
             for st, o in ((a_st, b), (r_st, s)):
                 re = [g[i] * o[i] + g[i + 2] * o[i + 2] for i in range(2)]
                 im = [g[i + 2] * o[i] - g[i] * o[i + 2] for i in range(2)]
-                st[at, :] = jnp.stack(re + im, 1).reshape(4 * SUB, 128)
+                for i, part in enumerate(re + im):
+                    st[chunk(k * SUB, SUB, i), :] = part
             return 0
 
-        lax.fori_loop(0, TILE // SUB, sub, 0)
+        lax.fori_loop(0, TILE // SUB, sub, 0, unroll=8)
 
         def scatter(g, _):
-            for j in range(UNROLL):
-                e = base + g * UNROLL + j
-                at, to = row(src[e]), row(rel[e])
-                gleft[at, :] = gleft[at, :] + a_st[spot(g, j), :]
-                grel[to, :] = grel[to, :] + r_st[spot(g, j), :]
+            at = [src[base + g * UNROLL + j] for j in range(UNROLL)]
+            to = [rel[base + g * UNROLL + j] for j in range(UNROLL)]
+            add_rows((gleft, at, staged(a_st, g)), (grel, to, staged(r_st, g)))
             return 0
 
         lax.fori_loop(0, groups, scatter, 0)
@@ -422,27 +437,30 @@
         copy.start()
         copy.wait()
 
-    def peer(back_ref, p, _):
+    def unpack(back_ref, p, _):
         parts = unpack_wire(back_ref[p].astype(F32))
-        stage[...] = jnp.stack(
-            [part.reshape(SLOT // 8, 8, 128) for part in parts], 1
-        ).reshape(4 * SLOT, 128)
+        for k, part in enumerate(parts):
+            stage[chunk(p * SLOT, SLOT, k), :] = part
+        return 0
+
+    def scatter(p, _):
         base = p * (SPANS * SLOT) + c * SLOT
 
-        def scatter(g, _):
-            for j in range(UNROLL):
-                at = row(ids[base + g * UNROLL + j])
-                total[at, :] = total[at, :] + stage[spot(g, j), :]
+        def group(g, _):
+            wanted = [ids[base + g * UNROLL + j] for j in range(UNROLL)]
+            add_rows((total, wanted, staged(stage, p * (SLOT // UNROLL) + g)))
             return 0
 
-        lax.fori_loop(0, SLOT // UNROLL, scatter, 0)
+        lax.fori_loop(0, SLOT // UNROLL, group, 0)
         return 0
 
     for k, back_ref in enumerate(backs):
 
         @pl.when(c // PART == k)
         def _():
-            lax.fori_loop(0, PEERS, functools.partial(peer, back_ref), 0)
+            lax.fori_loop(0, PEERS, functools.partial(unpack, back_ref), 0, unroll=4)
+
+    lax.fori_loop(0, PEERS, scatter, 0)
 
     @pl.when(c == SPANS - 1)
     def _():
@@ -473,7 +491,7 @@
         out_specs=[vmem] * 2,
         scratch_shapes=[
             pltpu.VMEM((TALL, 128), F32),
-            pltpu.VMEM((4 * SLOT, 128), F32),
+            pltpu.VMEM((PEERS * 4 * SLOT, 128), F32),
             pltpu.SemaphoreType.DMA,
         ],
         compiler_params=pltpu.CompilerParams(**PARAMS),
@@ -519,12 +537,10 @@
     return send
 
 
-def relation_sum_kernel(mine, out, got_0, half, got_1, sum_1, got_2, sum_2, sends, recvs):
+def relation_sum_kernel(mine, out, got_0, half, got_1, sends, recvs):
     core, chip, shard, other_core, along_grp, along_shard = places()
     steps = range(1, PEERS)
-    greet(
-        [other_core()] + [along_shard(d) for d in steps] + [along_grp(d) for d in steps]
-    )
+    greet([other_core()] + [along_shard(d) for d in steps])
     send = sender(sends, recvs)
     copy = send(mine.at[1 - core], got_0, 0, other_core())
     copy.wait()
@@ -545,24 +561,10 @@
         total = mine[core, shard, k].astype(F32) + got_0[shard, k].astype(F32)
         for d in range(PEERS - 1):
             total = total + got_1[d, k].astype(F32)
-        sum_1[k] = total
+        out[k] = total
         return 0
 
     lax.fori_loop(0, CHIPS, total_of, 0)
-    copies = [
-        send(sum_1.at[lax.rem(chip + d, CHIPS)], got_2.at[d - 1], 7 + d, along_grp(d))
-        for d in steps
-    ]
-    for copy in copies:
-        copy.wait()
-    total = sum_1[chip]
-    for d in range(CHIPS - 1):
-        total = total + got_2[d]
-    sum_2[...] = total
-    out[chip] = total
-    copies = [send(sum_2, out.at[chip], 14 + d, along_grp(d)) for d in steps]
-    for copy in copies:
-        copy.wait()
 
 
 def relation_sum(grad):
@@ -576,11 +578,8 @@
             pltpu.VMEM((PEERS, CHIPS, REL_SHARE, 128), BF16),
             pltpu.VMEM((PEERS, CHIPS, REL_SHARE, 128), BF16),
             pltpu.VMEM((PEERS - 1, CHIPS, REL_SHARE, 128), BF16),
-            pltpu.VMEM((CHIPS, REL_SHARE, 128), F32),
-            pltpu.VMEM((CHIPS - 1, REL_SHARE, 128), F32),
-            pltpu.VMEM((REL_SHARE, 128), F32),
-            pltpu.SemaphoreType.DMA((22,)),
-            pltpu.SemaphoreType.DMA((22,)),
+            pltpu.SemaphoreType.DMA((8,)),
+            pltpu.SemaphoreType.DMA((8,)),
         ],
         compiler_params=pltpu.CompilerParams(
             collective_id=0, has_side_effects=True, vmem_limit_bytes=32 * 1024 * 1024
@@ -588,6 +587,48 @@
         cost_estimate=pl.CostEstimate(flops=0, bytes_accessed=4_000_000, transcendentals=0),
         name="relation_sum",
     )(grad.reshape(CORES, PEERS, CHIPS, REL_SHARE, 128))
+
+
+def relation_cross_kernel(mine, out, got, total, sends, recvs):
+    core, chip, shard, other_core, along_grp, along_shard = places()
+    steps = range(1, CHIPS)
+    greet([along_grp(d) for d in steps])
+    send = sender(sends, recvs)
+    copies = [
+        send(mine.at[lax.rem(chip + d, CHIPS)], got.at[d - 1], d - 1, along_grp(d))
+        for d in steps
+    ]
+    for copy in copies:
+        copy.wait()
+    added = mine[chip]
+    for d in range(CHIPS - 1):
+        added = added + got[d]
+    total[...] = added
+    out[chip] = added
+    copies = [send(total, out.at[chip], 6 + d, along_grp(d)) for d in steps]
+    for copy in copies:
+        copy.wait()
+
+
+def relation_cross(share):
+    vmem = pl.BlockSpec(memory_space=pltpu.VMEM)
+    return pl.pallas_call(
+        relation_cross_kernel,
+        out_shape=jax.ShapeDtypeStruct((CHIPS, REL_SHARE, 128), F32),
+        in_specs=[vmem],
+        out_specs=vmem,
+        scratch_shapes=[
+            pltpu.VMEM((CHIPS - 1, REL_SHARE, 128), F32),
+            pltpu.VMEM((REL_SHARE, 128), F32),
+            pltpu.SemaphoreType.DMA((14,)),
+            pltpu.SemaphoreType.DMA((14,)),
+        ],
+        compiler_params=pltpu.CompilerParams(
+            collective_id=2, has_side_effects=True, vmem_limit_bytes=32 * 1024 * 1024
+        ),
+        cost_estimate=pl.CostEstimate(flops=0, bytes_accessed=4_000_000, transcendentals=0),
+        name="relation_cross",
+    )(share)
 
 
 def relation_spread_kernel(mine, out, sends, recvs):
@@ -686,23 +727,23 @@
     new_left, new_left_state, grad_rel = left_update(
         src, rel, live, source, relation, grad_product, left_t, left_state.reshape(1, ROWS)
     )
+    sent_left, grad_rel = lax.optimization_barrier((new_left.astype(jnp.float16), grad_rel))
+    moved_left = passed_along(sent_left, "grp", ROUND)
     rel_share = relation_sum(grad_rel)
-    sent_left, returned, rel_share = lax.optimization_barrier(
-        (new_left.astype(jnp.float16), returned, rel_share)
-    )
-    moved_left = passed_along(sent_left, "grp", ROUND)
+    returned, rel_share = lax.optimization_barrier((returned, rel_share))
     new_right, new_right_state = right_update(
         asked, returned, grad_right, right_t, right_state.reshape(1, ROWS)
     )
     rel_share, sent = lax.optimization_barrier((rel_share, new_right.astype(jnp.float16)))
+    rel_share = relation_cross(rel_share)
+    rel_share, sent = lax.optimization_barrier((rel_share, sent))
+    moved_right = passed_along(sent, "grp", ROUND)
     rel_total = relation_spread(rel_share)
-    moved_right = passed_along(sent, "grp", ROUND)
     states = jnp.concatenate([new_left_state, new_right_state], 0)
     moved_states = passed_along(states, "grp", ROUND)
     new_rel, new_rel_state = relation_update(rel_total, rel_t, rel_state.reshape(1, RELS_PAD))
-    new_rel, moved_left, moved_states = lax.optimization_barrier(
-        (new_rel, moved_left, moved_states)
-    )
+    new_rel, moved_left = lax.optimization_barrier((new_rel, moved_left))
+    moved_right, moved_states = lax.optimization_barrier((moved_right, moved_states))
     return (
         moved_left.astype(F32).T,
         moved_states[0],

time: 470 us -> 437 us (0.930)
  Pallas kernels: 383 us -> 338 us
  starting transfers between devices: 20.7 us -> 36.7 us
    pallas_call x1, Pallas kernels: 88.6 us -> 66.2 us  [forward(): pl.pallas_call(forward_kernel, grid=(SPANS,), out_shape=[per_edge] * 4 +...]
    ppermute x3, starting transfers between devices: 7.54 us -> 26.5 us  [passed_along(): return lax.ppermute(block, axis, route)]
    ppermute x3, waiting for transfers between devices: 25.4 us -> 10.5 us  [passed_along(): return lax.ppermute(block, axis, route)]
    pallas_call x1, Pallas kernels: 54.2 us -> 40.5 us  [relation_sum(): pl.pallas_call(relation_sum_kernel, out_shape=jax.ShapeDtypeStruct((CHIPS...]
    pallas_call x0 -> x1, Pallas kernels: none -> 12.9 us  [relation_cross(): pl.pallas_call(relation_cross_kernel, out_shape=jax.ShapeDtypeStruct((CHI...]
    all_to_all x2, waiting for transfers between devices: 0.01 us -> 11.8 us  [exchange(): return lax.all_to_all(x, 'shard', split_axis=0, concat_axis=0, tiled=True)]
    pallas_call x1, Pallas kernels: 53.2 us -> 43.7 us  [negatives(): pl.pallas_call(functools.partial(negatives_kernel, first), grid=(PART,),...]
    pallas_call x1, Pallas kernels: 33.6 us -> 25.8 us  [serve(): pl.pallas_call(serve_kernel, grid=(PEERS,), out_shape=jax.ShapeDtypeStruc...]
  transfers between devices with their start and end apart: 5 -> 5, of which waited for: 1 -> 2; matrix products, arithmetic and copies ran while one was open for 4% -> 4% of each run, Pallas kernels for 63% -> 61%
where the time goes in v2:
time: 437 us
  Pallas kernels  338 us (77%)
  starting transfers between devices  36.7 us (8%)
  waiting for transfers between devices  22.3 us (5%)
  other arithmetic  19.8 us (5%)
  blocking collectives  11.8 us (3%)
  local copies, waits for them, and re-layouts  7.4 us (2%)
    pallas_call x1, Pallas kernels, forward(): pl.pallas_call(forward_kernel, grid=(SPANS,), out_shape=[per_edge] * 4 +...  66.2 us
    pallas_call x1, Pallas kernels, relation_spread(): pl.pallas_call(relation_spread_kernel, out_shape=jax.ShapeDtypeStruct((CO...  54.6 us
    pallas_call x1, Pallas kernels, left_update(): pl.pallas_call(left_kernel, grid=(SPANS,), out_shape=[jax.ShapeDtypeStruc...  46.6 us
    pallas_call x1, Pallas kernels, negatives(): pl.pallas_call(functools.partial(negatives_kernel, first), grid=(PART,),...  43.7 us
    pallas_call x1, Pallas kernels, right_update(): pl.pallas_call(right_kernel, grid=(SPANS,), out_shape=[jax.ShapeDtypeStru...  42.8 us
    pallas_call x1, Pallas kernels, relation_sum(): pl.pallas_call(relation_sum_kernel, out_shape=jax.ShapeDtypeStruct((CHIPS...  40.5 us
    ppermute x3, starting transfers between devices, passed_along(): return lax.ppermute(block, axis, route)  26.5 us
    pallas_call x1, Pallas kernels, serve(): pl.pallas_call(serve_kernel, grid=(PEERS,), out_shape=jax.ShapeDtypeStruc...  25.8 us
  transfers between devices with their start and end apart: 5, of which 2 were waited for; matrix products, arithmetic and copies ran while one was open for 4% of the time, Pallas kernels for 61%

profile of v2, /device:TPU:1, one launch (start us, length us, event | category | flops | bytes accessed | tf_op | source)
XLA Modules:
  0.0 436.7 jit_solution(2079065191842347669)
XLA Ops:
  0.6 0.9 reshape.57
  1.6 11.8 %all_to_all.19 = s32[8,1,1152]{2,1,0:T(1,128)} all-to-all(s32[8,1,1152]{2,1,0:T(1,128)S(1)} %copy.17), channel_id=1, replica_groups=mesh['grp'=16,'shard'=8] {'shard'}, dimensions={0} | all-to-all | bytes 73728 | tf_op jit(solution)/shard_map/all_to_all | solution.py:699
  13.4 25.8 %serve.1 = bf16[8,3600,128]{2,1,0:T(8,128)(2,1)} custom-call(s32[9216]{0:T(1024)} %bitcast.27, f32[400,4096]{1,0:T(8,128)} %bitcast.21), custom_call_target="tpu_custom_call" | custom-call | bytes 80000000 | tf_op jit(solution)/shard_map/serve/pallas_call | solution.py:153
  39.3 0.0 copy-start.3
  39.3 0.0 copy-start.4
  39.3 0.0 copy-start.5
  39.3 0.0 copy-start.2
  39.3 5.0 %all-to-all-start.1 = ((bf16[8,3600,128]{2,1,0:T(8,128)(2,1)}), bf16[8,3600,128]{2,1,0:T(8,128)(2,1)}, u32[]{:S(2)}, u32[]{:S(2)}) async-start(bf16[8,3600,128]{2,1,0:T(8,128)(2,1)} %serve.1), calls=%async_computation.1 | async-start | bytes 14745600 | tf_op jit(solution)/shard_map/all_to_all | solution.py:699
  44.3 0.0 copy-done.3
  44.3 0.6 reshape.54.src
  44.9 0.0 copy-done.4
  44.9 0.6 reshape.55.rel
  45.5 0.0 copy-done.5
  45.6 0.6 reshape.56.tgt
  46.2 0.0 copy-done.2
  46.2 1.6 pad.25.rel_t
  47.8 66.2 %forward.1 = (bf16[9,1024,512]{2,1,0:T(8,128)(2,1)}, bf16[9,1024,512]{2,1,0:T(8,128)(2,1)}, bf16[9,1024,512]{2,1,0:T(8,128)(2,1)}, bf16[9,1024,512]{2,1,0:T(8,128)(2,1)}, f32[16384,128]{1,0:T(8,128)}) custom-call(s32[9216]{0:T(1024)} %reshape.54.src, s32[9216]{0:T(1024)} %reshape.55.rel, s32[9216]{0:T(1024)} %reshape.56.tgt, s32[9]{0:T(128)} %bitcast.34, ...), custom_call_target="tpu_custom_call" | custom-call | bytes 280000000 | tf_op jit(solution)/shard_map/forward/pallas_call | solution.py:257
  114.0 11.8 %all-to-all-done.1.got_ref = bf16[8,3600,128]{2,1,0:T(8,128)(2,1)} async-done(((bf16[8,3600,128]{2,1,0:T(8,128)(2,1)}), bf16[8,3600,128]{2,1,0:T(8,128)(2,1)}, u32[]{:S(2)}, u32[]{:S(2)}) %all-to-all-start.1) | async-done | bytes 7372832 | tf_op jit(solution)/shard_map/all_to_all | solution.py:699
  125.7 43.7 %negatives.1 = (bf16[9,1024,512]{2,1,0:T(8,128)(2,1)}, bf16[8,3600,128]{2,1,0:T(8,128)(2,1)}) custom-call(s32[9]{0:T(128)} %bitcast.35, bf16[9,1024,512]{2,1,0:T(8,128)(2,1)} %get-tuple-element.32.p_ref, bf16[9,1024,512]{2,1,0:T(8,128)(2,1)} %get-tuple-element.33.pt_ref, bf16[8,3600,128]{2,1,0:T(8,128)(2,1)} %all-to-all-done.1.got_ref), custom_call_target="tpu_custom_call" | custom-call | flops 14000000000 | bytes 60000000 | tf_op jit(solution)/shard_map/negatives/pallas_call | solution.py:337
  169.4 5.3 %all-to-all-start.2 = ((bf16[8,3600,128]{2,1,0:T(8,128)(2,1)}), bf16[8,3600,128]{2,1,0:T(8,128)(2,1)}, u32[]{:S(2)}, u32[]{:S(2)}) async-start(bf16[8,3600,128]{2,1,0:T(8,128)(2,1)} %get-tuple-element.34), calls=%async_computation.2 | async-start | bytes 14745600 | tf_op jit(solution)/shard_map/all_to_all | solution.py:699
  174.6 46.6 %left_update.1 = (f32[400,4096]{1,0:T(8,128)}, f32[1,4096]{1,0:T(1,128)}, bf16[6144,128]{1,0:T(8,128)(2,1)}) custom-call(s32[9216]{0:T(1024)} %reshape.54.src, s32[9216]{0:T(1024)} %reshape.55.rel, s32[9]{0:T(128)} %bitcast.36, bf16[9,1024,512]{2,1,0:T(8,128)(2,1)} %get-tuple-element.35.s_ref, bf16[9,1024,512]{2,1,0:T(8,128)(2,1)} %get-tuple-element.36.b_ref, ...), custom_call_target="tpu_custom_call" | custom-call | bytes 240000000 | tf_op jit(solution)/shard_map/left_update/pallas_call | solution.py:411
  221.2 0.0 copy-start.1
  221.2 5.1 %convert_element_type.10 = f16[400,4096]{1,0:T(8,128)(2,1)} convert(f32[400,4096]{1,0:T(8,128)} %get-tuple-element.38) | non-fusion elementwise | flops 1638400 | bytes 9830400 | tf_op jit(solution)/shard_map/convert_element_type | solution.py:730
  226.4 0.0 copy-done.1
  226.4 40.5 %relation_sum.1.mine = f32[8,48,128]{2,1,0:T(8,128)S(1)} custom-call(bf16[2,8,8,48,128]{4,3,2,1,0:T(8,128)(2,1)S(1)} %bitcast.20), custom_call_target="tpu_custom_call" | custom-call | bytes 4000000 | tf_op jit(solution)/shard_map/relation_sum/pallas_call | solution.py:572
  266.9 5.9 %collective-permute-start = (f16[400,4096]{1,0:T(8,128)(2,1)}, f16[400,4096]{1,0:T(8,128)(2,1)S(1)}, u32[]{:S(2)}, u32[]{:S(2)}) collective-permute-start(f16[400,4096]{1,0:T(8,128)(2,1)} %convert_element_type.10), channel_id=1, source_target_pairs={{88,0},{96,8},{104,16},{112,24},{120,32},{0,40},{8,48},{16,56},{24... | collective-permute-start | bytes 9830408 | tf_op jit(solution)/shard_map/ppermute | solution.py:695
  272.8 0.0 all-to-all-done.2.refs_0_
  272.8 42.8 %right_update.1 = (f32[400,4096]{1,0:T(8,128)}, f32[1,4096]{1,0:T(1,128)}) custom-call(s32[9216]{0:T(1024)} %bitcast.28, bf16[8,3600,128]{2,1,0:T(8,128)(2,1)} %all-to-all-done.2.refs_0_, f32[16384,128]{1,0:T(8,128)} %get-tuple-element.43.refs_1_, f32[400,4096]{1,0:T(8,128)} %bitcast.23, f32[1,4096]{1,0:T(1,128)} %bitcast.33), custom_call_target="tpu_custom_call" | custom-call | bytes 160000000 | tf_op jit(solution)/shard_map/right_update/pallas_call | solution.py:477
  315.6 0.0 copy-start.6
  315.6 0.0 copy-start.7
  315.6 0.0 copy-start.8
  315.6 5.1 %convert_element_type.11 = f16[400,4096]{1,0:T(8,128)(2,1)} convert(f32[400,4096]{1,0:T(8,128)} %get-tuple-element.44) | non-fusion elementwise | flops 1638400 | bytes 9830400 | tf_op jit(solution)/shard_map/convert_element_type | solution.py:737
  320.7 12.9 %relation_cross.1.mine = f32[8,48,128]{2,1,0:T(8,128)S(1)} custom-call(f32[8,48,128]{2,1,0:T(8,128)S(1)} %relation_sum.1.mine), custom_call_target="tpu_custom_call" | custom-call | bytes 4000000 | tf_op jit(solution)/shard_map/relation_cross/pallas_call | solution.py:615
  333.6 20.3 %collective-permute-start.1 = (f16[400,4096]{1,0:T(8,128)(2,1)}, f16[400,4096]{1,0:T(8,128)(2,1)}, u32[]{:S(2)}, u32[]{:S(2)}) collective-permute-start(f16[400,4096]{1,0:T(8,128)(2,1)} %convert_element_type.11), channel_id=1, source_target_pairs={{88,0},{96,8},{104,16},{112,24},{120,32},{0,40},{8,48},{16,56},{24... | collective-permute-start | bytes 9830408 | tf_op jit(solution)/shard_map/ppermute | solution.py:695
  353.9 0.0 copy-done.6
  353.9 0.0 copy-done.7
  353.9 0.3 collective-permute-start.2
  354.2 0.0 copy-done.8
  354.2 0.6 reshape.63.state
  354.8 54.6 %relation_spread.1 = f32[2,8,8,48,128]{4,3,2,1,0:T(8,128)S(1)} custom-call(f32[8,48,128]{2,1,0:T(8,128)S(1)} %relation_cross.1.mine), custom_call_target="tpu_custom_call" | custom-call | bytes 4000000 | tf_op jit(solution)/shard_map/relation_spread/pallas_call | solution.py:654
  409.4 0.0 copy-start
  409.4 1.7 copy-done
  411.1 4.9 %relation_update.1 = (f32[400,1345]{1,0:T(8,128)}, f32[1,1345]{1,0:T(1,128)}) custom-call(f32[6144,128]{1,0:T(8,128)} %bitcast.19, f32[400,1408]{1,0:T(8,128)} %pad.25.rel_t, f32[1,1408]{1,0:T(1,128)} %reshape.63.state), custom_call_target="tpu_custom_call" | custom-call | tf_op jit(solution)/shard_map/relation_update/pallas_call | solution.py:679
  416.0 0.0 collective-permute-done
  416.0 1.3 reduce
  417.3 10.5 %collective-permute-done.2 = f32[2,4096]{1,0:T(2,128)S(1)} collective-permute-done((f32[2,4096]{1,0:T(2,128)S(1)}, f32[2,4096]{1,0:T(2,128)S(1)}, u32[]{:S(2)}, u32[]{:S(2)}) %collective-permute-start.2) | collective-permute-done | bytes 32800 | tf_op jit(solution)/shard_map/ppermute | solution.py:695
  427.8 0.0 collective-permute-done.1
  427.8 0.6 fusion
  428.4 8.3 %convert_bitcast_fusion = (f32[4096,400]{0,1:T(8,128)}, f32[4096,400]{0,1:T(8,128)}) fusion(f16[400,4096]{1,0:T(8,128)(2,1)} %collective-permute-done.1, f16[400,4096]{1,0:T(8,128)(2,1)S(1)} %collective-permute-done), kind=kLoop, calls=%fused_computation | loop fusion | flops 3276800 | bytes 19660800 | tf_op jit(solution)/shard_map/transpose | solution.py:750
  (7 shorter events, 0.1 us)
Async XLA Ops:
  39.3 5.0 %copy-start.3 = (s32[9,1000]{1,0:T(8,128)S(1)}, s32[9,1000]{1,0:T(8,128)}, u32[]{:S(2)}) copy-start(s32[9,1000]{1,0:T(8,128)} %param.17) | copy-start | bytes 108004
  39.3 5.6 %copy-start.4 = (s32[9,1000]{1,0:T(8,128)S(1)}, s32[9,1000]{1,0:T(8,128)}, u32[]{:S(2)}) copy-start(s32[9,1000]{1,0:T(8,128)} %param.18) | copy-start | bytes 108004
  39.3 6.3 %copy-start.5 = (s32[9,1000]{1,0:T(8,128)S(1)}, s32[9,1000]{1,0:T(8,128)}, u32[]{:S(2)}) copy-start(s32[9,1000]{1,0:T(8,128)} %param.19) | copy-start | bytes 108004
  39.3 6.9 %copy-start.2 = (f32[1345,400]{0,1:T(8,128)S(1)}, f32[1345,400]{0,1:T(8,128)}, u32[]{:S(2)}) copy-start(f32[1345,400]{0,1:T(8,128)} %param.15) | copy-start | bytes 6456004
  39.3 86.4 %all-to-all-start.1 = ((bf16[8,3600,128]{2,1,0:T(8,128)(2,1)}), bf16[8,3600,128]{2,1,0:T(8,128)(2,1)}, u32[]{:S(2)}, u32[]{:S(2)}) async-start(bf16[8,3600,128]{2,1,0:T(8,128)(2,1)} %serve.1), calls=%async_computation.1 | async-start | bytes 14745600 | tf_op jit(solution)/shard_map/all_to_all | solution.py:699
  169.4 103.5 %all-to-all-start.2 = ((bf16[8,3600,128]{2,1,0:T(8,128)(2,1)}), bf16[8,3600,128]{2,1,0:T(8,128)(2,1)}, u32[]{:S(2)}, u32[]{:S(2)}) async-start(bf16[8,3600,128]{2,1,0:T(8,128)(2,1)} %get-tuple-element.34), calls=%async_computation.2 | async-start | bytes 14745600 | tf_op jit(solution)/shard_map/all_to_all | solution.py:699
  221.2 5.1 %copy-start.1 = (bf16[6144,128]{1,0:T(8,128)(2,1)S(1)}, bf16[6144,128]{1,0:T(8,128)(2,1)}, u32[]{:S(2)}) copy-start(bf16[6144,128]{1,0:T(8,128)(2,1)} %get-tuple-element.40) | copy-start | bytes 4718596
  266.9 149.1 %collective-permute-start = (f16[400,4096]{1,0:T(8,128)(2,1)}, f16[400,4096]{1,0:T(8,128)(2,1)S(1)}, u32[]{:S(2)}, u32[]{:S(2)}) collective-permute-start(f16[400,4096]{1,0:T(8,128)(2,1)} %convert_element_type.10), channel_id=1, source_target_pairs={{88,0},{96,8},{104,16},{112,24},{120,32},{0,40},{8,48},{16,56},{24... | collective-permute-start | bytes 9830408 | tf_op jit(solution)/shard_map/ppermute | solution.py:695
  315.6 38.3 %copy-start.6 = (f32[1,4096]{1,0:T(1,128)S(1)}, f32[1,4096]{1,0:T(1,128)}, u32[]{:S(2)}) copy-start(f32[1,4096]{1,0:T(1,128)} %get-tuple-element.52) | copy-start | bytes 49156
  315.6 38.3 %copy-start.7 = (f32[1,4096]{1,0:T(1,128)S(1)}, f32[1,4096]{1,0:T(1,128)}, u32[]{:S(2)}) copy-start(f32[1,4096]{1,0:T(1,128)} %get-tuple-element.53) | copy-start | bytes 49156
  315.6 38.6 %copy-start.8 = (f32[1345]{0:T(1024)S(1)}, f32[1345]{0:T(1024)}, u32[]{:S(2)}) copy-start(f32[1345]{0:T(1024)} %param.16) | copy-start | bytes 16144
  333.6 94.2 %collective-permute-start.1 = (f16[400,4096]{1,0:T(8,128)(2,1)}, f16[400,4096]{1,0:T(8,128)(2,1)}, u32[]{:S(2)}, u32[]{:S(2)}) collective-permute-start(f16[400,4096]{1,0:T(8,128)(2,1)} %convert_element_type.11), channel_id=1, source_target_pairs={{88,0},{96,8},{104,16},{112,24},{120,32},{0,40},{8,48},{16,56},{24... | collective-permute-start | bytes 9830408 | tf_op jit(solution)/shard_map/ppermute | solution.py:695
  353.9 73.9 %collective-permute-start.2 = (f32[2,4096]{1,0:T(2,128)S(1)}, f32[2,4096]{1,0:T(2,128)S(1)}, u32[]{:S(2)}, u32[]{:S(2)}) collective-permute-start(f32[2,4096]{1,0:T(2,128)S(1)} %pad_maximum_fusion), channel_id=1, source_target_pairs={{88,0},{96,8},{104,16},{112,24},{120,32},{0,40},{8,48},{16,56},{24... | collective-permute-start | bytes 98312 | tf_op jit(solution)/shard_map/ppermute | solution.py:695
  409.4 1.7 copy-start

commit v3 on v2

--- a/solution.py
+++ b/solution.py
@@ -28,8 +28,8 @@
 CHIPS = 8
 REL_SHARE = 48
 REL_TALL = CORES * PEERS * CHIPS * REL_SHARE
-PARTS = 1
-PART = SPANS // PARTS
+BOUNDS = (0, 3, SPANS)
+PARTS = len(BOUNDS) - 1
 TILE = 256
 SUB = 32
 UNROLL = 16
@@ -58,21 +58,24 @@
     lax.fori_loop(0, count // 128, block, 0, unroll=8 if count == ROWS else 1)
 
 
-def adagrad_block(g_ref, t, state, i):
+def adagrad_block(g_refs, t, state, i):
     parts = []
     for c, (low, high) in enumerate(CHUNKS):
-        part = g_ref[pl.ds(i * 512 + c, 128, stride=4), :].T
-        parts.append(part[: high - low])
+        at = pl.ds(i * 512 + c, 128, stride=4)
+        part = g_refs[0][at, :]
+        for g_ref in g_refs[1:]:
+            part = part + g_ref[at, :]
+        parts.append(part.T[: high - low])
     grad = jnp.concatenate(parts, 0)
     new_state = state + jnp.sum(grad * grad, 0, keepdims=True) * (1.0 / WIDTH)
     rate = LEARN_RATE / (jnp.sqrt(new_state) + EPSILON)
     return t - grad * rate, new_state
 
 
-def adagrad_tables(g_ref, t_ref, state_ref, new_ref, new_state_ref):
+def adagrad_tables(g_refs, t_ref, state_ref, new_ref, new_state_ref):
     def block(i, _):
         at = pl.ds(pl.multiple_of(i * 128, 128), 128)
-        new, state = adagrad_block(g_ref, t_ref[:, at], state_ref[:, at], i)
+        new, state = adagrad_block(g_refs, t_ref[:, at], state_ref[:, at], i)
         new_ref[:, at] = new.astype(new_ref.dtype)
         new_state_ref[:, at] = state
         return 0
@@ -92,21 +95,11 @@
     return pl.ds(pl.multiple_of(index * 4, 4), 4)
 
 
-TOGETHER = 1
-
-
 def add_rows(*work):
-    for first in range(0, len(work[0][1]), TOGETHER):
-        for ref, indices, values in work:
-            ids = indices[first : first + TOGETHER]
-            adds = [value() for value in values[first : first + TOGETHER]]
-            new = [ref[row(i), :] + add for i, add in zip(ids, adds)]
-            for k in range(len(ids)):
-                for j in range(k):
-                    same = jnp.where(ids[j] == ids[k], 1.0, 0.0)
-                    new[k] = new[k] + same * adds[j]
-            for i, value in zip(ids, new):
-                ref[row(i), :] = value
+    for j in range(len(work[0][1])):
+        for refs, indices, values in work:
+            ref, at = refs[j % len(refs)], row(indices[j])
+            ref[at, :] = ref[at, :] + values[j]()
 
 
 def staged(stage, group):
@@ -239,7 +232,7 @@
 
         def scatter(g, _):
             ids = [tgt[base + g * UNROLL + j] for j in range(UNROLL)]
-            add_rows((g_ref, ids, staged(g_st, g)))
+            add_rows(([g_ref], ids, staged(g_st, g)))
             return 0
 
         lax.fori_loop(0, groups, scatter, 0)
@@ -324,7 +317,7 @@
     lax.fori_loop(0, PEERS, pack, 0, unroll=4)
 
 
-def negatives(live, product, pos_target, got, first, grad_product):
+def negatives(live, product, pos_target, got, first, count, grad_product):
     block = pl.BlockSpec((1, SPAN_PAD, 512), lambda c: (first + c, 0, 0))
     wire = pl.BlockSpec((PEERS, WIRE, 128), lambda c: (0, first + c, 0))
     operands = [live, product, pos_target, got]
@@ -336,10 +329,10 @@
         aliases = {4: 0}
     return pl.pallas_call(
         functools.partial(negatives_kernel, first),
-        grid=(PART,),
+        grid=(count,),
         out_shape=[
             jax.ShapeDtypeStruct((SPANS, SPAN_PAD, 512), BF16),
-            jax.ShapeDtypeStruct((PEERS, PART * WIRE, 128), BF16),
+            jax.ShapeDtypeStruct((PEERS, count * WIRE, 128), BF16),
         ],
         in_specs=specs,
         out_specs=[block, pl.BlockSpec((PEERS, WIRE, 128), lambda c: (0, c, 0))],
@@ -350,21 +343,22 @@
         input_output_aliases=aliases,
         compiler_params=pltpu.CompilerParams(**PARAMS),
         cost_estimate=pl.CostEstimate(
-            flops=14_000_000_000, bytes_accessed=60_000_000, transcendentals=3_000_000
+            flops=5_000_000_000 * count, bytes_accessed=15_000_000 * count, transcendentals=0
         ),
         name="negatives",
     )(*operands)
 
 
 def left_kernel(
-    src, rel, live_ref, s_ref, b_ref, gp_ref, left_t, state, new_ref, new_state, rel_out, gleft, grel, a_st, r_st
+    src, rel, live_ref, s_ref, b_ref, gp_ref, left_t, state, new_ref, new_state, rel_out, *refs
 ):
+    glefts, grels, (a_st, r_st) = refs[:2], refs[2:4], refs[4:]
     c = pl.program_id(0)
 
     @pl.when(c == 0)
     def _():
-        gleft[...] = jnp.zeros_like(gleft)
-        grel[...] = jnp.zeros_like(grel)
+        for total in glefts + grels:
+            total[...] = jnp.zeros_like(total)
 
     live = live_ref[c]
 
@@ -390,7 +384,7 @@
         def scatter(g, _):
             at = [src[base + g * UNROLL + j] for j in range(UNROLL)]
             to = [rel[base + g * UNROLL + j] for j in range(UNROLL)]
-            add_rows((gleft, at, staged(a_st, g)), (grel, to, staged(r_st, g)))
+            add_rows((glefts, at, staged(a_st, g)), (grels, to, staged(r_st, g)))
             return 0
 
         lax.fori_loop(0, groups, scatter, 0)
@@ -400,8 +394,8 @@
 
     @pl.when(c == SPANS - 1)
     def _():
-        rel_out[...] = grel[...].astype(BF16)
-        adagrad_tables(gleft, left_t, state, new_ref, new_state)
+        rel_out[...] = (grels[0][...] + grels[1][...]).astype(BF16)
+        adagrad_tables(glefts, left_t, state, new_ref, new_state)
 
 
 def left_update(src, rel, live, source, relation, grad_product, left_t, state):
@@ -418,7 +412,8 @@
         ],
         in_specs=[smem] * 3 + [block] * 3 + [vmem] * 2,
         out_specs=[vmem] * 3,
-        scratch_shapes=[pltpu.VMEM((4 * ROWS, 128), F32), pltpu.VMEM((REL_TALL, 128), F32)]
+        scratch_shapes=[pltpu.VMEM((4 * ROWS, 128), F32)] * 2
+        + [pltpu.VMEM((REL_TALL, 128), F32)] * 2
         + [pltpu.VMEM((4 * TILE, 128), F32)] * 2,
         compiler_params=pltpu.CompilerParams(**PARAMS),
         cost_estimate=pl.CostEstimate(flops=0, bytes_accessed=240_000_000, transcendentals=0),
@@ -428,13 +423,14 @@
 
 def right_kernel(ids, *refs):
     backs = refs[:PARTS]
-    g_hbm, right_t, state, new_ref, new_state, total, stage, sem = refs[PARTS:]
+    g_hbm, right_t, state, new_ref, new_state, total, other, stage, sem = refs[PARTS:]
     c = pl.program_id(0)
 
     @pl.when(c == 0)
     def _():
         copy = pltpu.make_async_copy(g_hbm, total.at[pl.ds(0, 4 * ROWS)], sem)
         copy.start()
+        other[...] = jnp.zeros_like(other)
         copy.wait()
 
     def unpack(back_ref, p, _):
@@ -448,7 +444,7 @@
 
         def group(g, _):
             wanted = [ids[base + g * UNROLL + j] for j in range(UNROLL)]
-            add_rows((total, wanted, staged(stage, p * (SLOT // UNROLL) + g)))
+            add_rows(([total, other], wanted, staged(stage, p * (SLOT // UNROLL) + g)))
             return 0
 
         lax.fori_loop(0, SLOT // UNROLL, group, 0)
@@ -456,7 +452,7 @@
 
     for k, back_ref in enumerate(backs):
 
-        @pl.when(c // PART == k)
+        @pl.when((c >= BOUNDS[k]) & (c < BOUNDS[k + 1]))
         def _():
             lax.fori_loop(0, PEERS, functools.partial(unpack, back_ref), 0, unroll=4)
 
@@ -464,13 +460,14 @@
 
     @pl.when(c == SPANS - 1)
     def _():
-        adagrad_tables(total, right_t, state, new_ref, new_state)
+        adagrad_tables([total, other], right_t, state, new_ref, new_state)
 
 
 def right_update(ids, backs, grad, right_t, state):
     def part(k):
         return pl.BlockSpec(
-            (PEERS, WIRE, 128), lambda c: (0, jnp.clip(c - k * PART, 0, PART - 1), 0)
+            (PEERS, WIRE, 128),
+            lambda c: (0, jnp.clip(c - BOUNDS[k], 0, BOUNDS[k + 1] - BOUNDS[k] - 1), 0),
         )
 
     vmem = pl.BlockSpec(memory_space=pltpu.VMEM)
@@ -491,11 +488,12 @@
         out_specs=[vmem] * 2,
         scratch_shapes=[
             pltpu.VMEM((TALL, 128), F32),
+            pltpu.VMEM((TALL, 128), F32),
             pltpu.VMEM((PEERS * 4 * SLOT, 128), F32),
             pltpu.SemaphoreType.DMA,
         ],
         compiler_params=pltpu.CompilerParams(**PARAMS),
-        cost_estimate=pl.CostEstimate(flops=0, bytes_accessed=160_000_000, transcendentals=0),
+        cost_estimate=pl.CostEstimate(flops=0, bytes_accessed=4_000_000, transcendentals=0),
         name="right_update",
     )(ids, *backs, grad, right_t, state)
 
@@ -537,10 +535,12 @@
     return send
 
 
-def relation_sum_kernel(mine, out, got_0, half, got_1, sends, recvs):
+def relation_sum_kernel(mine, out, got_0, half, got_1, sum_1, got_2, sum_2, sends, recvs):
     core, chip, shard, other_core, along_grp, along_shard = places()
     steps = range(1, PEERS)
-    greet([other_core()] + [along_shard(d) for d in steps])
+    greet(
+        [other_core()] + [along_shard(d) for d in steps] + [along_grp(d) for d in steps]
+    )
     send = sender(sends, recvs)
     copy = send(mine.at[1 - core], got_0, 0, other_core())
     copy.wait()
@@ -561,10 +561,24 @@
         total = mine[core, shard, k].astype(F32) + got_0[shard, k].astype(F32)
         for d in range(PEERS - 1):
             total = total + got_1[d, k].astype(F32)
-        out[k] = total
+        sum_1[k] = total
         return 0
 
     lax.fori_loop(0, CHIPS, total_of, 0)
+    copies = [
+        send(sum_1.at[lax.rem(chip + d, CHIPS)], got_2.at[d - 1], 7 + d, along_grp(d))
+        for d in steps
+    ]
+    for copy in copies:
+        copy.wait()
+    total = sum_1[chip]
+    for d in range(CHIPS - 1):
+        total = total + got_2[d]
+    sum_2[...] = total
+    out[chip] = total
+    copies = [send(sum_2, out.at[chip], 14 + d, along_grp(d)) for d in steps]
+    for copy in copies:
+        copy.wait()
 
 
 def relation_sum(grad):
@@ -578,8 +592,11 @@
             pltpu.VMEM((PEERS, CHIPS, REL_SHARE, 128), BF16),
             pltpu.VMEM((PEERS, CHIPS, REL_SHARE, 128), BF16),
             pltpu.VMEM((PEERS - 1, CHIPS, REL_SHARE, 128), BF16),
-            pltpu.SemaphoreType.DMA((8,)),
-            pltpu.SemaphoreType.DMA((8,)),
+            pltpu.VMEM((CHIPS, REL_SHARE, 128), F32),
+            pltpu.VMEM((CHIPS - 1, REL_SHARE, 128), F32),
+            pltpu.VMEM((REL_SHARE, 128), F32),
+            pltpu.SemaphoreType.DMA((22,)),
+            pltpu.SemaphoreType.DMA((22,)),
         ],
         compiler_params=pltpu.CompilerParams(
             collective_id=0, has_side_effects=True, vmem_limit_bytes=32 * 1024 * 1024
@@ -587,48 +604,6 @@
         cost_estimate=pl.CostEstimate(flops=0, bytes_accessed=4_000_000, transcendentals=0),
         name="relation_sum",
     )(grad.reshape(CORES, PEERS, CHIPS, REL_SHARE, 128))
-
-
-def relation_cross_kernel(mine, out, got, total, sends, recvs):
-    core, chip, shard, other_core, along_grp, along_shard = places()
-    steps = range(1, CHIPS)
-    greet([along_grp(d) for d in steps])
-    send = sender(sends, recvs)
-    copies = [
-        send(mine.at[lax.rem(chip + d, CHIPS)], got.at[d - 1], d - 1, along_grp(d))
-        for d in steps
-    ]
-    for copy in copies:
-        copy.wait()
-    added = mine[chip]
-    for d in range(CHIPS - 1):
-        added = added + got[d]
-    total[...] = added
-    out[chip] = added
-    copies = [send(total, out.at[chip], 6 + d, along_grp(d)) for d in steps]
-    for copy in copies:
-        copy.wait()
-
-
-def relation_cross(share):
-    vmem = pl.BlockSpec(memory_space=pltpu.VMEM)
-    return pl.pallas_call(
-        relation_cross_kernel,
-        out_shape=jax.ShapeDtypeStruct((CHIPS, REL_SHARE, 128), F32),
-        in_specs=[vmem],
-        out_specs=vmem,
-        scratch_shapes=[
-            pltpu.VMEM((CHIPS - 1, REL_SHARE, 128), F32),
-            pltpu.VMEM((REL_SHARE, 128), F32),
-            pltpu.SemaphoreType.DMA((14,)),
-            pltpu.SemaphoreType.DMA((14,)),
-        ],
-        compiler_params=pltpu.CompilerParams(
-            collective_id=2, has_side_effects=True, vmem_limit_bytes=32 * 1024 * 1024
-        ),
-        cost_estimate=pl.CostEstimate(flops=0, bytes_accessed=4_000_000, transcendentals=0),
-        name="relation_cross",
-    )(share)
 
 
 def relation_spread_kernel(mine, out, sends, recvs):
@@ -669,7 +644,7 @@
 def relation_kernel(g_ref, rel_t, state, new_ref, new_state):
     for i in range(RELS_PAD // 128):
         low, high = i * 128, min(RELS, i * 128 + 128)
-        new, ns = adagrad_block(g_ref, rel_t[:, low : low + 128], state[:, low : low + 128], i)
+        new, ns = adagrad_block([g_ref], rel_t[:, low : low + 128], state[:, low : low + 128], i)
         new_ref[:, low:high] = new[:, : high - low]
         new_state[:, low:high] = ns[:, : high - low]
 
@@ -721,31 +696,34 @@
         src, rel, tgt, live, left_t, right_t, rel_t
     )
     grad_product, returned = None, []
-    for k in range(PARTS):
-        grad_product, back = negatives(live, product, pos_target, got, k * PART, grad_product)
+    for first, end in zip(BOUNDS, BOUNDS[1:]):
+        grad_product, back = negatives(
+            live, product, pos_target, got, first, end - first, grad_product
+        )
+        if returned:
+            returned[-1], back = lax.optimization_barrier((returned[-1], back))
         returned.append(exchange(back))
     new_left, new_left_state, grad_rel = left_update(
         src, rel, live, source, relation, grad_product, left_t, left_state.reshape(1, ROWS)
     )
-    sent_left, grad_rel = lax.optimization_barrier((new_left.astype(jnp.float16), grad_rel))
-    moved_left = passed_along(sent_left, "grp", ROUND)
-    rel_share = relation_sum(grad_rel)
-    returned, rel_share = lax.optimization_barrier((returned, rel_share))
+    moved_left = passed_along(new_left.astype(jnp.float16), "grp", ROUND)
     new_right, new_right_state = right_update(
         asked, returned, grad_right, right_t, right_state.reshape(1, ROWS)
     )
-    rel_share, sent = lax.optimization_barrier((rel_share, new_right.astype(jnp.float16)))
-    rel_share = relation_cross(rel_share)
+    grad_rel, sent = lax.optimization_barrier((grad_rel, new_right.astype(jnp.float16)))
+    rel_share = relation_sum(grad_rel)
     rel_share, sent = lax.optimization_barrier((rel_share, sent))
     moved_right = passed_along(sent, "grp", ROUND)
     rel_total = relation_spread(rel_share)
     states = jnp.concatenate([new_left_state, new_right_state], 0)
     moved_states = passed_along(states, "grp", ROUND)
+    held_left, rel_total = lax.optimization_barrier((moved_left.astype(F32), rel_total))
     new_rel, new_rel_state = relation_update(rel_total, rel_t, rel_state.reshape(1, RELS_PAD))
-    new_rel, moved_left = lax.optimization_barrier((new_rel, moved_left))
-    moved_right, moved_states = lax.optimization_barrier((moved_right, moved_states))
+    moved_right, moved_states, new_rel = lax.optimization_barrier(
+        (moved_right, moved_states, new_rel)
+    )
     return (
-        moved_left.astype(F32).T,
+        held_left.T,
         moved_states[0],
         moved_right.astype(F32).T,
         moved_states[1],

time: 437 us -> 399 us (0.913)
  Pallas kernels: 338 us -> 314 us
  starting transfers between devices: 36.7 us -> 25.4 us
    ppermute x3, starting transfers between devices: 26.5 us -> 10.9 us  [passed_along(): return lax.ppermute(block, axis, route)]
    pallas_call x2, Pallas kernels: 56.5 us -> 49.2 us  [negatives(): pl.pallas_call(functools.partial(negatives_kernel, first), grid=(count,),...]
    pallas_call x1, Pallas kernels: 46.6 us -> 40.7 us  [left_update(): pl.pallas_call(left_kernel, grid=(SPANS,), out_shape=[jax.ShapeDtypeStruc...]
    convert_element_type x1 -> x2, other arithmetic: 5.14 us -> 10.3 us  [the longest x1 5.27 us: local(): moved_left.astype(F32)]
    pallas_call x1, Pallas kernels: 54.6 us -> 49.5 us  [relation_spread(): pl.pallas_call(relation_spread_kernel, out_shape=jax.ShapeDtypeStruct((CO...]
    all_to_all x2 -> x3, starting transfers between devices: 10.2 us -> 14.5 us  [exchange(): return lax.all_to_all(x, 'shard', split_axis=0, concat_axis=0, tiled=True)]
    all_to_all x2 -> x3, waiting for transfers between devices: 11.8 us -> 10.3 us  [exchange(): return lax.all_to_all(x, 'shard', split_axis=0, concat_axis=0, tiled=True)]
  transfers between devices with their start and end apart: 5 -> 6, of which waited for: 2 -> 2; matrix products, arithmetic and copies ran while one was open for 4% -> 5% of each run, Pallas kernels for 61% -> 68%
where the time goes in v3:
time: 399 us; the launch traced here: 398 us
  Pallas kernels  314 us (79%)
  starting transfers between devices  25.4 us (6%)
  other arithmetic  20.4 us (5%)
  waiting for transfers between devices  18.7 us (5%)
  blocking collectives  11.8 us (3%)
  local copies, waits for them, and re-layouts  7.35 us (2%)
    pallas_call x1, Pallas kernels, forward(): pl.pallas_call(forward_kernel, grid=(SPANS,), out_shape=[per_edge] * 4 +...  67.6 us
    pallas_call x1, Pallas kernels, relation_spread(): pl.pallas_call(relation_spread_kernel, out_shape=jax.ShapeDtypeStruct((CO...  49.5 us
    pallas_call x2, Pallas kernels, negatives(): pl.pallas_call(functools.partial(negatives_kernel, first), grid=(count,),...  49.2 us
    pallas_call x1, Pallas kernels, left_update(): pl.pallas_call(left_kernel, grid=(SPANS,), out_shape=[jax.ShapeDtypeStruc...  40.7 us
    pallas_call x1, Pallas kernels, right_update(): pl.pallas_call(right_kernel, grid=(SPANS,), out_shape=[jax.ShapeDtypeStru...  39.6 us
    pallas_call x1, Pallas kernels, relation_sum(): pl.pallas_call(relation_sum_kernel, out_shape=jax.ShapeDtypeStruct((CHIPS...  36.6 us
    pallas_call x1, Pallas kernels, serve(): pl.pallas_call(serve_kernel, grid=(PEERS,), out_shape=jax.ShapeDtypeStruc...  25.9 us
    all_to_all x3, starting transfers between devices, exchange(): return lax.all_to_all(x, 'shard', split_axis=0, concat_axis=0, tiled=True)  14.5 us
  transfers between devices with their start and end apart: 6, of which 2 were waited for; matrix products, arithmetic and copies ran while one was open for 5% of the time, Pallas kernels for 68%

profile of v3, /device:TPU:1, one launch (start us, length us, event | category | flops | bytes accessed | tf_op | source)
XLA Modules:
  0.0 398.5 jit_solution(1109782134209487456)
XLA Ops:
  0.6 0.9 reshape.57
  1.6 11.8 %all_to_all.24 = s32[8,1,1152]{2,1,0:T(1,128)} all-to-all(s32[8,1,1152]{2,1,0:T(1,128)S(1)} %copy.18), channel_id=1, replica_groups=mesh['grp'=16,'shard'=8] {'shard'}, dimensions={0} | all-to-all | bytes 73728 | tf_op jit(solution)/shard_map/all_to_all | solution.py:674
  13.4 25.9 %serve.1 = bf16[8,3600,128]{2,1,0:T(8,128)(2,1)} custom-call(s32[9216]{0:T(1024)} %bitcast.27, f32[400,4096]{1,0:T(8,128)} %bitcast.20), custom_call_target="tpu_custom_call" | custom-call | bytes 80000000 | tf_op jit(solution)/shard_map/serve/pallas_call | solution.py:146
  39.3 0.0 copy-start.4
  39.3 0.0 copy-start.5
  39.3 0.0 copy-start.6
  39.3 0.0 copy-start.3
  39.3 5.0 %all-to-all-start.1 = ((bf16[8,3600,128]{2,1,0:T(8,128)(2,1)}), bf16[8,3600,128]{2,1,0:T(8,128)(2,1)}, u32[]{:S(2)}, u32[]{:S(2)}) async-start(bf16[8,3600,128]{2,1,0:T(8,128)(2,1)} %serve.1), calls=%async_computation.1 | async-start | bytes 14745600 | tf_op jit(solution)/shard_map/all_to_all | solution.py:674
  44.3 0.0 copy-done.4
  44.3 0.6 reshape.53.src
  44.9 0.0 copy-done.5
  44.9 0.6 reshape.54.rel
  45.6 0.0 copy-done.6
  45.6 0.6 reshape.56.tgt
  46.2 0.0 copy-done.3
  46.2 1.5 pad.25.rel_t
  47.8 67.6 %forward.1 = (bf16[9,1024,512]{2,1,0:T(8,128)(2,1)}, bf16[9,1024,512]{2,1,0:T(8,128)(2,1)}, bf16[9,1024,512]{2,1,0:T(8,128)(2,1)}, bf16[9,1024,512]{2,1,0:T(8,128)(2,1)}, f32[16384,128]{1,0:T(8,128)}) custom-call(s32[9216]{0:T(1024)} %reshape.53.src, s32[9216]{0:T(1024)} %reshape.54.rel, s32[9216]{0:T(1024)} %reshape.56.tgt, s32[9]{0:T(128)} %bitcast.34, ...), custom_call_target="tpu_custom_call" | custom-call | bytes 280000000 | tf_op jit(solution)/shard_map/forward/pallas_call | solution.py:250
  115.4 10.3 %all-to-all-done.1.got_ref = bf16[8,3600,128]{2,1,0:T(8,128)(2,1)} async-done(((bf16[8,3600,128]{2,1,0:T(8,128)(2,1)}), bf16[8,3600,128]{2,1,0:T(8,128)(2,1)}, u32[]{:S(2)}, u32[]{:S(2)}) %all-to-all-start.1) | async-done | bytes 7372832 | tf_op jit(solution)/shard_map/all_to_all | solution.py:674
  125.7 19.1 %negatives.2 = (bf16[9,1024,512]{2,1,0:T(8,128)(2,1)}, bf16[8,1200,128]{2,1,0:T(8,128)(2,1)}) custom-call(s32[9]{0:T(128)} %bitcast.35, bf16[9,1024,512]{2,1,0:T(8,128)(2,1)} %get-tuple-element.35.p_ref, bf16[9,1024,512]{2,1,0:T(8,128)(2,1)} %get-tuple-element.36.pt_ref, bf16[8,3600,128]{2,1,0:T(8,128)(2,1)} %all-to-all-done.1.got_ref), custom_call_target="tpu_custom_call" | custom-call | flops 15000000512 | bytes 45000000 | tf_op jit(solution)/shard_map/negatives/pallas_call | solution.py:330
  144.8 3.6 all-to-all-start.2
  148.4 30.1 %negatives.3 = (bf16[9,1024,512]{2,1,0:T(8,128)(2,1)}, bf16[8,2400,128]{2,1,0:T(8,128)(2,1)}) custom-call(s32[9]{0:T(128)} %bitcast.36, bf16[9,1024,512]{2,1,0:T(8,128)(2,1)} %get-tuple-element.35.p_ref, bf16[9,1024,512]{2,1,0:T(8,128)(2,1)} %get-tuple-element.36.pt_ref, ...), custom_call_target="tpu_custom_call", output_to_operand_aliasing={{0}: (4, {})} | custom-call | flops 30000001024 | bytes 90000000 | tf_op jit(solution)/shard_map/negatives/pallas_call | solution.py:330
  178.5 0.0 all-to-all-done.2.refs_0_
  178.5 0.0 copy-start.2
  178.6 5.9 %all-to-all-start.3 = ((bf16[8,2400,128]{2,1,0:T(8,128)(2,1)}), bf16[8,2400,128]{2,1,0:T(8,128)(2,1)}, u32[]{:S(2)}, u32[]{:S(2)}) async-start(bf16[8,2400,128]{2,1,0:T(8,128)(2,1)} %get-tuple-element.44), calls=%async_computation.3 | async-start | bytes 9830400 | tf_op jit(solution)/shard_map/all_to_all | solution.py:674
  184.4 40.7 %left_update.1 = (f32[400,4096]{1,0:T(8,128)}, f32[1,4096]{1,0:T(1,128)}, bf16[6144,128]{1,0:T(8,128)(2,1)}) custom-call(s32[9216]{0:T(1024)} %reshape.53.src, s32[9216]{0:T(1024)} %reshape.54.rel, s32[9]{0:T(128)} %bitcast.37, bf16[9,1024,512]{2,1,0:T(8,128)(2,1)} %get-tuple-element.33.s_ref, bf16[9,1024,512]{2,1,0:T(8,128)(2,1)} %get-tuple-element.34.b_ref, ...), custom_call_target="tpu_custom_call" | custom-call | bytes 240000000 | tf_op jit(solution)/shard_map/left_update/pallas_call | solution.py:405
  225.2 0.0 copy-done.2
  225.2 5.0 %convert_element_type.12 = f16[400,4096]{1,0:T(8,128)(2,1)} convert(f32[400,4096]{1,0:T(8,128)} %get-tuple-element.39) | non-fusion elementwise | flops 1638400 | bytes 9830400 | tf_op jit(solution)/shard_map/convert_element_type | solution.py:709
  230.2 6.9 %collective-permute-start = (f16[400,4096]{1,0:T(8,128)(2,1)}, f16[400,4096]{1,0:T(8,128)(2,1)}, u32[]{:S(2)}, u32[]{:S(2)}) collective-permute-start(f16[400,4096]{1,0:T(8,128)(2,1)} %convert_element_type.12), channel_id=1, source_target_pairs={{88,0},{96,8},{104,16},{112,24},{120,32},{0,40},{8,48},{16,56},{24... | collective-permute-start | bytes 9830408 | tf_op jit(solution)/shard_map/ppermute | solution.py:670
  237.1 0.0 all-to-all-done.3.refs_1_
  237.1 39.6 %right_update.1 = (f32[400,4096]{1,0:T(8,128)}, f32[1,4096]{1,0:T(1,128)}) custom-call(s32[9216]{0:T(1024)} %bitcast.28, bf16[8,1200,128]{2,1,0:T(8,128)(2,1)} %copy-done.2, bf16[8,2400,128]{2,1,0:T(8,128)(2,1)} %all-to-all-done.3.refs_1_, f32[16384,128]{1,0:T(8,128)} %get-tuple-element.45.refs_2_, f32[400,4096]{1,0:T(8,128)} %bitcast.22, f32[1,4096]{1,0:T(1,128)} %bitcast.33), custom_call_target="tpu_custom_call" | custom-call | bytes 4000000 | tf_op jit(solution)/shard_map/right_update/pallas_call | solution.py:474
  276.7 0.0 copy-start.1
  276.7 0.0 copy-start.7
  276.7 0.0 copy-start.8
  276.7 0.0 copy-start.9
  276.7 3.5 convert_element_type.14
  280.2 0.0 copy-done.1
  280.2 36.6 %relation_sum.1.mine = f32[8,48,128]{2,1,0:T(8,128)S(1)} custom-call(bf16[2,8,8,48,128]{4,3,2,1,0:T(8,128)(2,1)S(1)} %bitcast.19), custom_call_target="tpu_custom_call" | custom-call | bytes 4000000 | tf_op jit(solution)/shard_map/relation_sum/pallas_call | solution.py:586
  316.8 3.9 collective-permute-start.1
  320.7 0.0 copy-done.7
  320.7 0.0 copy-done.8
  320.8 0.1 collective-permute-start.2
  320.9 0.0 copy-done.9
  320.9 0.6 reshape.63.state
  321.5 0.0 collective-permute-done
  321.5 5.3 %convert_element_type.13 = f32[400,4096]{1,0:T(8,128)} convert(f16[400,4096]{1,0:T(8,128)(2,1)} %collective-permute-done) | non-fusion elementwise | flops 1638400 | bytes 9830400 | tf_op jit(solution)/shard_map/convert_element_type | solution.py:720
  326.7 49.5 %relation_spread.1 = f32[2,8,8,48,128]{4,3,2,1,0:T(8,128)S(1)} custom-call(f32[8,48,128]{2,1,0:T(8,128)S(1)} %relation_sum.1.mine), custom_call_target="tpu_custom_call" | custom-call | bytes 4000000 | tf_op jit(solution)/shard_map/relation_spread/pallas_call | solution.py:629
  376.3 0.0 copy-start
  376.3 1.7 copy-done
  378.0 4.9 %relation_update.1 = (f32[400,1345]{1,0:T(8,128)}, f32[1,1345]{1,0:T(1,128)}) custom-call(f32[6144,128]{1,0:T(8,128)} %bitcast.18, f32[400,1408]{1,0:T(8,128)} %pad.25.rel_t, f32[1,1408]{1,0:T(1,128)} %reshape.63.state), custom_call_target="tpu_custom_call" | custom-call | tf_op jit(solution)/shard_map/relation_update/pallas_call | solution.py:654
  382.9 1.3 reduce
  384.2 8.4 %collective-permute-done.2 = f32[2,4096]{1,0:T(2,128)S(1)} collective-permute-done((f32[2,4096]{1,0:T(2,128)S(1)}, f32[2,4096]{1,0:T(2,128)S(1)}, u32[]{:S(2)}, u32[]{:S(2)}) %collective-permute-start.2) | collective-permute-done | bytes 32800 | tf_op jit(solution)/shard_map/ppermute | solution.py:670
  392.6 0.0 collective-permute-done.1
  392.6 5.3 %convert_bitcast_fusion = f32[4096,400]{0,1:T(8,128)} fusion(f16[400,4096]{1,0:T(8,128)(2,1)} %collective-permute-done.1), kind=kLoop, calls=%fused_computation | loop fusion | flops 1638400 | bytes 9830400 | tf_op jit(solution)/shard_map/transpose | solution.py:728
  397.8 0.6 fusion
  (7 shorter events, 0.1 us)
Async XLA Ops:
  39.3 5.0 %copy-start.4 = (s32[9,1000]{1,0:T(8,128)S(1)}, s32[9,1000]{1,0:T(8,128)}, u32[]{:S(2)}) copy-start(s32[9,1000]{1,0:T(8,128)} %param.17) | copy-start | bytes 108004
  39.3 5.6 %copy-start.5 = (s32[9,1000]{1,0:T(8,128)S(1)}, s32[9,1000]{1,0:T(8,128)}, u32[]{:S(2)}) copy-start(s32[9,1000]{1,0:T(8,128)} %param.18) | copy-start | bytes 108004
  39.3 6.3 %copy-start.6 = (s32[9,1000]{1,0:T(8,128)S(1)}, s32[9,1000]{1,0:T(8,128)}, u32[]{:S(2)}) copy-start(s32[9,1000]{1,0:T(8,128)} %param.19) | copy-start | bytes 108004
  39.3 6.9 %copy-start.3 = (f32[1345,400]{0,1:T(8,128)S(1)}, f32[1345,400]{0,1:T(8,128)}, u32[]{:S(2)}) copy-start(f32[1345,400]{0,1:T(8,128)} %param.15) | copy-start | bytes 6456004
  39.3 86.4 %all-to-all-start.1 = ((bf16[8,3600,128]{2,1,0:T(8,128)(2,1)}), bf16[8,3600,128]{2,1,0:T(8,128)(2,1)}, u32[]{:S(2)}, u32[]{:S(2)}) async-start(bf16[8,3600,128]{2,1,0:T(8,128)(2,1)} %serve.1), calls=%async_computation.1 | async-start | bytes 14745600 | tf_op jit(solution)/shard_map/all_to_all | solution.py:674
  144.8 33.7 %all-to-all-start.2 = ((bf16[8,1200,128]{2,1,0:T(8,128)(2,1)}), bf16[8,1200,128]{2,1,0:T(8,128)(2,1)S(1)}, u32[]{:S(2)}, u32[]{:S(2)}) async-start(bf16[8,1200,128]{2,1,0:T(8,128)(2,1)} %get-tuple-element.41), calls=%async_computation.2 | async-start | bytes 4915200 | tf_op jit(solution)/shard_map/all_to_all | solution.py:674
  178.5 46.6 %copy-start.2 = (bf16[8,1200,128]{2,1,0:T(8,128)(2,1)}, bf16[8,1200,128]{2,1,0:T(8,128)(2,1)S(1)}, u32[]{:S(2)}) copy-start(bf16[8,1200,128]{2,1,0:T(8,128)(2,1)S(1)} %all-to-all-done.2.refs_0_) | copy-start | bytes 7372804
  178.6 58.5 %all-to-all-start.3 = ((bf16[8,2400,128]{2,1,0:T(8,128)(2,1)}), bf16[8,2400,128]{2,1,0:T(8,128)(2,1)}, u32[]{:S(2)}, u32[]{:S(2)}) async-start(bf16[8,2400,128]{2,1,0:T(8,128)(2,1)} %get-tuple-element.44), calls=%async_computation.3 | async-start | bytes 9830400 | tf_op jit(solution)/shard_map/all_to_all | solution.py:674
  230.2 91.3 %collective-permute-start = (f16[400,4096]{1,0:T(8,128)(2,1)}, f16[400,4096]{1,0:T(8,128)(2,1)}, u32[]{:S(2)}, u32[]{:S(2)}) collective-permute-start(f16[400,4096]{1,0:T(8,128)(2,1)} %convert_element_type.12), channel_id=1, source_target_pairs={{88,0},{96,8},{104,16},{112,24},{120,32},{0,40},{8,48},{16,56},{24... | collective-permute-start | bytes 9830408 | tf_op jit(solution)/shard_map/ppermute | solution.py:670
  276.7 3.5 copy-start.1
  276.7 44.0 %copy-start.7 = (f32[1,4096]{1,0:T(1,128)S(1)}, f32[1,4096]{1,0:T(1,128)}, u32[]{:S(2)}) copy-start(f32[1,4096]{1,0:T(1,128)} %get-tuple-element.52) | copy-start | bytes 49156
  276.7 44.0 %copy-start.8 = (f32[1,4096]{1,0:T(1,128)S(1)}, f32[1,4096]{1,0:T(1,128)}, u32[]{:S(2)}) copy-start(f32[1,4096]{1,0:T(1,128)} %get-tuple-element.53) | copy-start | bytes 49156
  276.7 44.2 %copy-start.9 = (f32[1345]{0:T(1024)S(1)}, f32[1345]{0:T(1024)}, u32[]{:S(2)}) copy-start(f32[1345]{0:T(1024)} %param.16) | copy-start | bytes 16144
  316.8 75.8 %collective-permute-start.1 = (f16[400,4096]{1,0:T(8,128)(2,1)S(1)}, f16[400,4096]{1,0:T(8,128)(2,1)}, u32[]{:S(2)}, u32[]{:S(2)}) collective-permute-start(f16[400,4096]{1,0:T(8,128)(2,1)S(1)} %convert_element_type.14), channel_id=1, source_target_pairs={{88,0},{96,8},{104,16},{112,24},{120,32},{0,40},{8,48},{16,56},{24... | collective-permute-start | bytes 9830408 | tf_op jit(solution)/shard_map/ppermute | solution.py:670
  320.8 71.8 %collective-permute-start.2 = (f32[2,4096]{1,0:T(2,128)S(1)}, f32[2,4096]{1,0:T(2,128)S(1)}, u32[]{:S(2)}, u32[]{:S(2)}) collective-permute-start(f32[2,4096]{1,0:T(2,128)S(1)} %pad_maximum_fusion), channel_id=1, source_target_pairs={{88,0},{96,8},{104,16},{112,24},{120,32},{0,40},{8,48},{16,56},{24... | collective-permute-start | bytes 98312 | tf_op jit(solution)/shard_map/ppermute | solution.py:670
  376.3 1.7 copy-start

commit v4 on v3

--- a/solution.py
+++ b/solution.py
@@ -350,13 +350,15 @@
 
 
 def left_kernel(
-    src, rel, live_ref, s_ref, b_ref, gp_ref, left_t, state, new_ref, new_state, rel_out, *refs
+    src, rel, live_ref, s_ref, b_ref, gp_ref, left_hbm, state, new_ref, new_state, rel_out, *refs
 ):
-    glefts, grels, (a_st, r_st) = refs[:2], refs[2:4], refs[4:]
+    glefts, grels, (a_st, r_st, left_t, sem) = refs[:2], refs[2:4], refs[4:]
+    table = pltpu.make_async_copy(left_hbm, left_t, sem)
     c = pl.program_id(0)
 
     @pl.when(c == 0)
     def _():
+        table.start()
         for total in glefts + grels:
             total[...] = jnp.zeros_like(total)
 
@@ -395,6 +397,7 @@
     @pl.when(c == SPANS - 1)
     def _():
         rel_out[...] = (grels[0][...] + grels[1][...]).astype(BF16)
+        table.wait()
         adagrad_tables(glefts, left_t, state, new_ref, new_state)
 
 
@@ -410,11 +413,12 @@
             jax.ShapeDtypeStruct((1, ROWS), F32),
             jax.ShapeDtypeStruct((REL_TALL, 128), BF16),
         ],
-        in_specs=[smem] * 3 + [block] * 3 + [vmem] * 2,
+        in_specs=[smem] * 3 + [block] * 3 + [pl.BlockSpec(memory_space=pl.ANY), vmem],
         out_specs=[vmem] * 3,
         scratch_shapes=[pltpu.VMEM((4 * ROWS, 128), F32)] * 2
         + [pltpu.VMEM((REL_TALL, 128), F32)] * 2
-        + [pltpu.VMEM((4 * TILE, 128), F32)] * 2,
+        + [pltpu.VMEM((4 * TILE, 128), F32)] * 2
+        + [pltpu.VMEM((WIDTH, ROWS), F32), pltpu.SemaphoreType.DMA],
         compiler_params=pltpu.CompilerParams(**PARAMS),
         cost_estimate=pl.CostEstimate(flops=0, bytes_accessed=240_000_000, transcendentals=0),
         name="left_update",
@@ -423,7 +427,9 @@
 
 def right_kernel(ids, *refs):
     backs = refs[:PARTS]
-    g_hbm, right_t, state, new_ref, new_state, total, other, stage, sem = refs[PARTS:]
+    g_hbm, right_hbm, state, new_ref, new_state = refs[PARTS : PARTS + 5]
+    total, other, stage, sem, right_t, table_sem = refs[PARTS + 5 :]
+    table = pltpu.make_async_copy(right_hbm, right_t, table_sem)
     c = pl.program_id(0)
 
     @pl.when(c == 0)
@@ -432,6 +438,7 @@
         copy.start()
         other[...] = jnp.zeros_like(other)
         copy.wait()
+        table.start()
 
     def unpack(back_ref, p, _):
         parts = unpack_wire(back_ref[p].astype(F32))
@@ -460,6 +467,7 @@
 
     @pl.when(c == SPANS - 1)
     def _():
+        table.wait()
         adagrad_tables([total, other], right_t, state, new_ref, new_state)
 
 
@@ -482,7 +490,7 @@
             pl.BlockSpec(memory_space=pltpu.SMEM),
             *(part(k) for k in range(PARTS)),
             pl.BlockSpec(memory_space=pl.ANY),
-            vmem,
+            pl.BlockSpec(memory_space=pl.ANY),
             vmem,
         ],
         out_specs=[vmem] * 2,
@@ -490,6 +498,8 @@
             pltpu.VMEM((TALL, 128), F32),
             pltpu.VMEM((TALL, 128), F32),
             pltpu.VMEM((PEERS * 4 * SLOT, 128), F32),
+            pltpu.SemaphoreType.DMA,
+            pltpu.VMEM((WIDTH, ROWS), F32),
             pltpu.SemaphoreType.DMA,
         ],
         compiler_params=pltpu.CompilerParams(**PARAMS),

time: 399 us -> 398 us (level)
  Pallas kernels: 314 us -> 304 us
  waiting for transfers between devices: 18.7 us -> 23.8 us
  starting transfers between devices: 25.4 us -> 29.9 us
    all_to_all x3, waiting for transfers between devices: 10.3 us -> 16 us  [exchange(): return lax.all_to_all(x, 'shard', split_axis=0, concat_axis=0, tiled=True)]
  transfers between devices with their start and end apart: 6 -> 6, of which waited for: 2 -> 3; matrix products, arithmetic and copies ran while one was open for 5% -> 5% of each run, Pallas kernels for 68% -> 66%
where the time goes in v4:
time: 398 us
  Pallas kernels  304 us (76%)
  starting transfers between devices  29.9 us (8%)
  waiting for transfers between devices  23.8 us (6%)
  other arithmetic  20.4 us (5%)
  blocking collectives  11.8 us (3%)
  local copies, waits for them, and re-layouts  7.35 us (2%)
    pallas_call x1, Pallas kernels, forward(): pl.pallas_call(forward_kernel, grid=(SPANS,), out_shape=[per_edge] * 4 +...  66.2 us
    pallas_call x1, Pallas kernels, relation_spread(): pl.pallas_call(relation_spread_kernel, out_shape=jax.ShapeDtypeStruct((CO...  49.8 us
    pallas_call x2, Pallas kernels, negatives(): pl.pallas_call(functools.partial(negatives_kernel, first), grid=(count,),...  47.8 us
    pallas_call x1, Pallas kernels, left_update(): pl.pallas_call(left_kernel, grid=(SPANS,), out_shape=[jax.ShapeDtypeStruc...  37.8 us
    pallas_call x1, Pallas kernels, right_update(): pl.pallas_call(right_kernel, grid=(SPANS,), out_shape=[jax.ShapeDtypeStru...  37.6 us
    pallas_call x1, Pallas kernels, relation_sum(): pl.pallas_call(relation_sum_kernel, out_shape=jax.ShapeDtypeStruct((CHIPS...  34.3 us
    pallas_call x1, Pallas kernels, serve(): pl.pallas_call(serve_kernel, grid=(PEERS,), out_shape=jax.ShapeDtypeStruc...  25.9 us
    all_to_all x3, starting transfers between devices, exchange(): return lax.all_to_all(x, 'shard', split_axis=0, concat_axis=0, tiled=True)  17.8 us
  transfers between devices with their start and end apart: 6, of which 3 were waited for; matrix products, arithmetic and copies ran while one was open for 5% of the time, Pallas kernels for 66%

profile of v4, /device:TPU:1, one launch (start us, length us, event | category | flops | bytes accessed | tf_op | source)
XLA Modules:
  0.0 398.3 jit_solution(5743594988269974079)
XLA Ops:
  0.6 0.9 reshape.57
  1.6 11.8 %all_to_all.24 = s32[8,1,1152]{2,1,0:T(1,128)} all-to-all(s32[8,1,1152]{2,1,0:T(1,128)S(1)} %copy.18), channel_id=1, replica_groups=mesh['grp'=16,'shard'=8] {'shard'}, dimensions={0} | all-to-all | bytes 73728 | tf_op jit(solution)/shard_map/all_to_all | solution.py:684
  13.4 25.9 %serve.1 = bf16[8,3600,128]{2,1,0:T(8,128)(2,1)} custom-call(s32[9216]{0:T(1024)} %bitcast.27, f32[400,4096]{1,0:T(8,128)} %bitcast.20), custom_call_target="tpu_custom_call" | custom-call | bytes 80000000 | tf_op jit(solution)/shard_map/serve/pallas_call | solution.py:146
  39.3 0.0 copy-start.4
  39.3 0.0 copy-start.5
  39.3 0.0 copy-start.6
  39.3 0.0 copy-start.3
  39.3 5.0 %all-to-all-start.1 = ((bf16[8,3600,128]{2,1,0:T(8,128)(2,1)}), bf16[8,3600,128]{2,1,0:T(8,128)(2,1)}, u32[]{:S(2)}, u32[]{:S(2)}) async-start(bf16[8,3600,128]{2,1,0:T(8,128)(2,1)} %serve.1), calls=%async_computation.1 | async-start | bytes 14745600 | tf_op jit(solution)/shard_map/all_to_all | solution.py:684
  44.3 0.0 copy-done.4
  44.3 0.6 reshape.53.src
  44.9 0.0 copy-done.5
  44.9 0.6 reshape.54.rel
  45.6 0.0 copy-done.6
  45.6 0.6 reshape.56.tgt
  46.2 0.0 copy-done.3
  46.2 1.5 pad.25.rel_t
  47.8 66.2 %forward.1 = (bf16[9,1024,512]{2,1,0:T(8,128)(2,1)}, bf16[9,1024,512]{2,1,0:T(8,128)(2,1)}, bf16[9,1024,512]{2,1,0:T(8,128)(2,1)}, bf16[9,1024,512]{2,1,0:T(8,128)(2,1)}, f32[16384,128]{1,0:T(8,128)}) custom-call(s32[9216]{0:T(1024)} %reshape.53.src, s32[9216]{0:T(1024)} %reshape.54.rel, s32[9216]{0:T(1024)} %reshape.56.tgt, s32[9]{0:T(128)} %bitcast.34, ...), custom_call_target="tpu_custom_call" | custom-call | bytes 280000000 | tf_op jit(solution)/shard_map/forward/pallas_call | solution.py:250
  114.0 11.8 %all-to-all-done.1.got_ref = bf16[8,3600,128]{2,1,0:T(8,128)(2,1)} async-done(((bf16[8,3600,128]{2,1,0:T(8,128)(2,1)}), bf16[8,3600,128]{2,1,0:T(8,128)(2,1)}, u32[]{:S(2)}, u32[]{:S(2)}) %all-to-all-start.1) | async-done | bytes 7372832 | tf_op jit(solution)/shard_map/all_to_all | solution.py:684
  125.7 15.8 %negatives.2 = (bf16[9,1024,512]{2,1,0:T(8,128)(2,1)}, bf16[8,1200,128]{2,1,0:T(8,128)(2,1)}) custom-call(s32[9]{0:T(128)} %bitcast.35, bf16[9,1024,512]{2,1,0:T(8,128)(2,1)} %get-tuple-element.35.p_ref, bf16[9,1024,512]{2,1,0:T(8,128)(2,1)} %get-tuple-element.36.pt_ref, bf16[8,3600,128]{2,1,0:T(8,128)(2,1)} %all-to-all-done.1.got_ref), custom_call_target="tpu_custom_call" | custom-call | flops 15000000512 | bytes 45000000 | tf_op jit(solution)/shard_map/negatives/pallas_call | solution.py:330
  141.5 8.2 %all-to-all-start.2 = ((bf16[8,1200,128]{2,1,0:T(8,128)(2,1)}), bf16[8,1200,128]{2,1,0:T(8,128)(2,1)S(1)}, u32[]{:S(2)}, u32[]{:S(2)}) async-start(bf16[8,1200,128]{2,1,0:T(8,128)(2,1)} %get-tuple-element.41), calls=%async_computation.2 | async-start | bytes 4915200 | tf_op jit(solution)/shard_map/all_to_all | solution.py:684
  149.7 32.0 %negatives.3 = (bf16[9,1024,512]{2,1,0:T(8,128)(2,1)}, bf16[8,2400,128]{2,1,0:T(8,128)(2,1)}) custom-call(s32[9]{0:T(128)} %bitcast.36, bf16[9,1024,512]{2,1,0:T(8,128)(2,1)} %get-tuple-element.35.p_ref, bf16[9,1024,512]{2,1,0:T(8,128)(2,1)} %get-tuple-element.36.pt_ref, ...), custom_call_target="tpu_custom_call", output_to_operand_aliasing={{0}: (4, {})} | custom-call | flops 30000001024 | bytes 90000000 | tf_op jit(solution)/shard_map/negatives/pallas_call | solution.py:330
  181.7 0.0 all-to-all-done.2.refs_0_
  181.7 0.0 copy-start.2
  181.7 4.6 %all-to-all-start.3 = ((bf16[8,2400,128]{2,1,0:T(8,128)(2,1)}), bf16[8,2400,128]{2,1,0:T(8,128)(2,1)}, u32[]{:S(2)}, u32[]{:S(2)}) async-start(bf16[8,2400,128]{2,1,0:T(8,128)(2,1)} %get-tuple-element.44), calls=%async_computation.3 | async-start | bytes 9830400 | tf_op jit(solution)/shard_map/all_to_all | solution.py:684
  186.4 37.8 %left_update.1 = (f32[400,4096]{1,0:T(8,128)}, f32[1,4096]{1,0:T(1,128)}, bf16[6144,128]{1,0:T(8,128)(2,1)}) custom-call(s32[9216]{0:T(1024)} %reshape.53.src, s32[9216]{0:T(1024)} %reshape.54.rel, s32[9]{0:T(128)} %bitcast.37, bf16[9,1024,512]{2,1,0:T(8,128)(2,1)} %get-tuple-element.33.s_ref, bf16[9,1024,512]{2,1,0:T(8,128)(2,1)} %get-tuple-element.34.b_ref, ...), custom_call_target="tpu_custom_call" | custom-call | bytes 240000000 | tf_op jit(solution)/shard_map/left_update/pallas_call | solution.py:408
  224.2 0.0 copy-done.2
  224.2 5.0 %convert_element_type.12 = f16[400,4096]{1,0:T(8,128)(2,1)} convert(f32[400,4096]{1,0:T(8,128)} %get-tuple-element.39) | non-fusion elementwise | flops 1638400 | bytes 9830400 | tf_op jit(solution)/shard_map/convert_element_type | solution.py:719
  229.2 7.9 %collective-permute-start = (f16[400,4096]{1,0:T(8,128)(2,1)}, f16[400,4096]{1,0:T(8,128)(2,1)}, u32[]{:S(2)}, u32[]{:S(2)}) collective-permute-start(f16[400,4096]{1,0:T(8,128)(2,1)} %convert_element_type.12), channel_id=1, source_target_pairs={{88,0},{96,8},{104,16},{112,24},{120,32},{0,40},{8,48},{16,56},{24... | collective-permute-start | bytes 9830408 | tf_op jit(solution)/shard_map/ppermute | solution.py:680
  237.2 4.2 %all-to-all-done.3.refs_1_ = bf16[8,2400,128]{2,1,0:T(8,128)(2,1)} async-done(((bf16[8,2400,128]{2,1,0:T(8,128)(2,1)}), bf16[8,2400,128]{2,1,0:T(8,128)(2,1)}, u32[]{:S(2)}, u32[]{:S(2)}) %all-to-all-start.3) | async-done | bytes 4915232 | tf_op jit(solution)/shard_map/all_to_all | solution.py:684
  241.4 37.6 %right_update.1 = (f32[400,4096]{1,0:T(8,128)}, f32[1,4096]{1,0:T(1,128)}) custom-call(s32[9216]{0:T(1024)} %bitcast.28, bf16[8,1200,128]{2,1,0:T(8,128)(2,1)} %copy-done.2, bf16[8,2400,128]{2,1,0:T(8,128)(2,1)} %all-to-all-done.3.refs_1_, f32[16384,128]{1,0:T(8,128)} %get-tuple-element.45.refs_2_, f32[400,4096]{1,0:T(8,128)} %bitcast.22, f32[1,4096]{1,0:T(1,128)} %bitcast.33), custom_call_target="tpu_custom_call" | custom-call | bytes 4000000 | tf_op jit(solution)/shard_map/right_update/pallas_call | solution.py:482
  279.0 0.0 copy-start.1
  279.0 0.0 copy-start.7
  279.0 0.0 copy-start.8
  279.0 0.0 copy-start.9
  279.0 3.5 convert_element_type.14
  282.5 0.0 copy-done.1
  282.5 34.3 %relation_sum.1.mine = f32[8,48,128]{2,1,0:T(8,128)S(1)} custom-call(bf16[2,8,8,48,128]{4,3,2,1,0:T(8,128)(2,1)S(1)} %bitcast.19), custom_call_target="tpu_custom_call" | custom-call | bytes 4000000 | tf_op jit(solution)/shard_map/relation_sum/pallas_call | solution.py:596
  316.8 4.0 %collective-permute-start.1 = (f16[400,4096]{1,0:T(8,128)(2,1)S(1)}, f16[400,4096]{1,0:T(8,128)(2,1)}, u32[]{:S(2)}, u32[]{:S(2)}) collective-permute-start(f16[400,4096]{1,0:T(8,128)(2,1)S(1)} %convert_element_type.14), channel_id=1, source_target_pairs={{88,0},{96,8},{104,16},{112,24},{120,32},{0,40},{8,48},{16,56},{24... | collective-permute-start | bytes 9830408 | tf_op jit(solution)/shard_map/ppermute | solution.py:680
  320.8 0.0 copy-done.7
  320.8 0.0 copy-done.8
  320.9 0.1 collective-permute-start.2
  321.0 0.0 copy-done.9
  321.0 0.6 reshape.63.state
  321.6 0.0 collective-permute-done
  321.6 5.3 %convert_element_type.13 = f32[400,4096]{1,0:T(8,128)} convert(f16[400,4096]{1,0:T(8,128)(2,1)} %collective-permute-done) | non-fusion elementwise | flops 1638400 | bytes 9830400 | tf_op jit(solution)/shard_map/convert_element_type | solution.py:730
  326.8 49.8 %relation_spread.1 = f32[2,8,8,48,128]{4,3,2,1,0:T(8,128)S(1)} custom-call(f32[8,48,128]{2,1,0:T(8,128)S(1)} %relation_sum.1.mine), custom_call_target="tpu_custom_call" | custom-call | bytes 4000000 | tf_op jit(solution)/shard_map/relation_spread/pallas_call | solution.py:639
  376.7 0.0 copy-start
  376.7 1.7 copy-done
  378.3 4.9 %relation_update.1 = (f32[400,1345]{1,0:T(8,128)}, f32[1,1345]{1,0:T(1,128)}) custom-call(f32[6144,128]{1,0:T(8,128)} %bitcast.18, f32[400,1408]{1,0:T(8,128)} %pad.25.rel_t, f32[1,1408]{1,0:T(1,128)} %reshape.63.state), custom_call_target="tpu_custom_call" | custom-call | tf_op jit(solution)/shard_map/relation_update/pallas_call | solution.py:664
  383.2 1.3 reduce
  384.6 7.8 %collective-permute-done.2 = f32[2,4096]{1,0:T(2,128)S(1)} collective-permute-done((f32[2,4096]{1,0:T(2,128)S(1)}, f32[2,4096]{1,0:T(2,128)S(1)}, u32[]{:S(2)}, u32[]{:S(2)}) %collective-permute-start.2) | collective-permute-done | bytes 32800 | tf_op jit(solution)/shard_map/ppermute | solution.py:680
  392.4 0.0 collective-permute-done.1
  392.4 5.3 %convert_bitcast_fusion = f32[4096,400]{0,1:T(8,128)} fusion(f16[400,4096]{1,0:T(8,128)(2,1)} %collective-permute-done.1), kind=kLoop, calls=%fused_computation | loop fusion | flops 1638400 | bytes 9830400 | tf_op jit(solution)/shard_map/transpose | solution.py:738
  397.6 0.6 fusion
  (7 shorter events, 0.1 us)
Async XLA Ops:
  39.3 5.0 %copy-start.4 = (s32[9,1000]{1,0:T(8,128)S(1)}, s32[9,1000]{1,0:T(8,128)}, u32[]{:S(2)}) copy-start(s32[9,1000]{1,0:T(8,128)} %param.17) | copy-start | bytes 108004
  39.3 5.6 %copy-start.5 = (s32[9,1000]{1,0:T(8,128)S(1)}, s32[9,1000]{1,0:T(8,128)}, u32[]{:S(2)}) copy-start(s32[9,1000]{1,0:T(8,128)} %param.18) | copy-start | bytes 108004
  39.3 6.3 %copy-start.6 = (s32[9,1000]{1,0:T(8,128)S(1)}, s32[9,1000]{1,0:T(8,128)}, u32[]{:S(2)}) copy-start(s32[9,1000]{1,0:T(8,128)} %param.19) | copy-start | bytes 108004
  39.3 6.9 %copy-start.3 = (f32[1345,400]{0,1:T(8,128)S(1)}, f32[1345,400]{0,1:T(8,128)}, u32[]{:S(2)}) copy-start(f32[1345,400]{0,1:T(8,128)} %param.15) | copy-start | bytes 6456004
  39.3 86.4 %all-to-all-start.1 = ((bf16[8,3600,128]{2,1,0:T(8,128)(2,1)}), bf16[8,3600,128]{2,1,0:T(8,128)(2,1)}, u32[]{:S(2)}, u32[]{:S(2)}) async-start(bf16[8,3600,128]{2,1,0:T(8,128)(2,1)} %serve.1), calls=%async_computation.1 | async-start | bytes 14745600 | tf_op jit(solution)/shard_map/all_to_all | solution.py:684
  141.5 40.2 %all-to-all-start.2 = ((bf16[8,1200,128]{2,1,0:T(8,128)(2,1)}), bf16[8,1200,128]{2,1,0:T(8,128)(2,1)S(1)}, u32[]{:S(2)}, u32[]{:S(2)}) async-start(bf16[8,1200,128]{2,1,0:T(8,128)(2,1)} %get-tuple-element.41), calls=%async_computation.2 | async-start | bytes 4915200 | tf_op jit(solution)/shard_map/all_to_all | solution.py:684
  181.7 42.5 %copy-start.2 = (bf16[8,1200,128]{2,1,0:T(8,128)(2,1)}, bf16[8,1200,128]{2,1,0:T(8,128)(2,1)S(1)}, u32[]{:S(2)}) copy-start(bf16[8,1200,128]{2,1,0:T(8,128)(2,1)S(1)} %all-to-all-done.2.refs_0_) | copy-start | bytes 7372804
  181.7 59.7 %all-to-all-start.3 = ((bf16[8,2400,128]{2,1,0:T(8,128)(2,1)}), bf16[8,2400,128]{2,1,0:T(8,128)(2,1)}, u32[]{:S(2)}, u32[]{:S(2)}) async-start(bf16[8,2400,128]{2,1,0:T(8,128)(2,1)} %get-tuple-element.44), calls=%async_computation.3 | async-start | bytes 9830400 | tf_op jit(solution)/shard_map/all_to_all | solution.py:684
  229.2 92.4 %collective-permute-start = (f16[400,4096]{1,0:T(8,128)(2,1)}, f16[400,4096]{1,0:T(8,128)(2,1)}, u32[]{:S(2)}, u32[]{:S(2)}) collective-permute-start(f16[400,4096]{1,0:T(8,128)(2,1)} %convert_element_type.12), channel_id=1, source_target_pairs={{88,0},{96,8},{104,16},{112,24},{120,32},{0,40},{8,48},{16,56},{24... | collective-permute-start | bytes 9830408 | tf_op jit(solution)/shard_map/ppermute | solution.py:680
  279.0 3.5 copy-start.1
  279.0 41.8 %copy-start.7 = (f32[1,4096]{1,0:T(1,128)S(1)}, f32[1,4096]{1,0:T(1,128)}, u32[]{:S(2)}) copy-start(f32[1,4096]{1,0:T(1,128)} %get-tuple-element.52) | copy-start | bytes 49156
  279.0 41.8 %copy-start.8 = (f32[1,4096]{1,0:T(1,128)S(1)}, f32[1,4096]{1,0:T(1,128)}, u32[]{:S(2)}) copy-start(f32[1,4096]{1,0:T(1,128)} %get-tuple-element.53) | copy-start | bytes 49156
  279.0 41.9 %copy-start.9 = (f32[1345]{0:T(1024)S(1)}, f32[1345]{0:T(1024)}, u32[]{:S(2)}) copy-start(f32[1345]{0:T(1024)} %param.16) | copy-start | bytes 16144
  316.8 75.6 %collective-permute-start.1 = (f16[400,4096]{1,0:T(8,128)(2,1)S(1)}, f16[400,4096]{1,0:T(8,128)(2,1)}, u32[]{:S(2)}, u32[]{:S(2)}) collective-permute-start(f16[400,4096]{1,0:T(8,128)(2,1)S(1)} %convert_element_type.14), channel_id=1, source_target_pairs={{88,0},{96,8},{104,16},{112,24},{120,32},{0,40},{8,48},{16,56},{24... | collective-permute-start | bytes 9830408 | tf_op jit(solution)/shard_map/ppermute | solution.py:680
  320.9 71.5 %collective-permute-start.2 = (f32[2,4096]{1,0:T(2,128)S(1)}, f32[2,4096]{1,0:T(2,128)S(1)}, u32[]{:S(2)}, u32[]{:S(2)}) collective-permute-start(f32[2,4096]{1,0:T(2,128)S(1)} %pad_maximum_fusion), channel_id=1, source_target_pairs={{88,0},{96,8},{104,16},{112,24},{120,32},{0,40},{8,48},{16,56},{24... | collective-permute-start | bytes 98312 | tf_op jit(solution)/shard_map/ppermute | solution.py:680
  376.7 1.7 copy-start
